TPU v7x, 256 devices: a whole 4x4x8 slice. The times are simulated.
256 devices in a mesh: row: 8 (over x, core), col: 32 (over z, y).
Axes of the slice: x: 4, y: 4, z: 8, core: 2. Of those that a mesh axis runs over, the one named last changes fastest.
Arguments:
- tokens: bfloat16 [128, 8192], P('row', 'col'), may hold values from -7 to 7
- cotangent: bfloat16 [128, 8192], P('row', 'col'), may hold values from -7 to 7
- gate_weight: bfloat16 [8192, 28672], P('col', 'row'), may hold values from -0.0625 to 0.0625
- up_weight: bfloat16 [8192, 28672], P('col', 'row'), may hold values from -0.0625 to 0.0625
- down_weight: bfloat16 [28672, 8192], P('row', 'col'), may hold values from -0.03125 to 0.03125
- coefficients: float32 [2, 1000], replicated, may hold values from -4 to 4
- spectral_rows: int32 [2, 1000], replicated, may hold values from 0 to 28671, as said below
- spectral_cols: int32 [2, 1000], replicated, may hold values from 0 to 28671, as said below
- adam_first: float32 [2, 1000], replicated, may hold values from -0.0234375 to 0.0234375
- adam_second: float32 [2, 1000], replicated, may hold values from 2e-07 to 5e-06
Outputs:
- mixed: bfloat16 [128, 8192], P('row', 'col')
- adam_step: float32 [2, 1000], replicated
Inputs may be any that keep to these rules, and one draw needn't show every extreme that they name: `spectral_rows`: row 0 lies below 8192, row 1 below 28672. `spectral_cols`: row 0 lies below 28672, row 1 below 8192.
All inputs are finite; a program needn't handle non-finite values.
Results may differ from a plain program's by a relative error of at most 0.015.
Values may be sent and summed in bfloat16 or wider, within the bound.
No kernel may reach another device: no remote copies, remote signals or barrier semaphores. Data moves between devices by JAX's collectives and lax.ppermute only.
A program may use at most 128 MiB of HBM per device.

v0:
```python
import math

import jax
import jax.numpy as jnp
from jax import lax
from jax.experimental import pallas as pl
from jax.experimental.pallas import tpu as pltpu
from jax.sharding import Mesh
from jax.sharding import PartitionSpec as P

D = 8192
FF = 28672
N_COEF = 1000
ADAM_STEP = 3
PAD = 1024
SCALE_UP = 1.0 / math.sqrt(2.0 * D * N_COEF)
SCALE_DOWN = 1.0 / math.sqrt(2.0 * FF * N_COEF)
TWO_PI = 6.283185307179586

F32 = jnp.float32
BF16 = jnp.bfloat16
LOW = 8
MID = 16
SPAN = LOW * MID

PLANE = ("x", "core")
VMEM = pl.BlockSpec(memory_space=pltpu.VMEM)


def params(mib):
    return pltpu.CompilerParams(vmem_limit_bytes=mib << 20)


def waves(index, freq, width, axis):
    phase = index[..., None] * freq % width
    angle = phase.astype(F32) * (TWO_PI / width)
    return jnp.stack([jnp.cos(angle), jnp.sin(angle)], axis=axis)


def phases(freq, first, blocks, width):
    rows = -(-(LOW + MID + blocks) // 8) * 8
    index = jnp.concatenate(
        [
            jnp.arange(LOW, dtype=jnp.int32),
            LOW * jnp.arange(MID, dtype=jnp.int32),
            first + SPAN * jnp.arange(blocks, dtype=jnp.int32),
            jnp.zeros(rows - LOW - MID - blocks, jnp.int32),
        ]
    )
    return waves(index, freq, width, 0)


def span_table(cos, sin):
    low_cos, low_sin = cos[:LOW], sin[:LOW]
    out_cos, out_sin = [], []
    for k in range(MID):
        a, b = cos[LOW + k : LOW + k + 1], sin[LOW + k : LOW + k + 1]
        out_cos.append(a * low_cos - b * low_sin)
        out_sin.append(b * low_cos + a * low_sin)
    return jnp.concatenate(out_cos, axis=0), jnp.concatenate(out_sin, axis=0)


def turned(cos, sin, span_cos, span_sin):
    return cos * span_cos - sin * span_sin, sin * span_cos + cos * span_sin


def against(left, table):
    return lax.dot_general(
        left, table, (((1,), (1,)), ((), ())), preferred_element_type=F32
    )


def matmul(left, right):
    return jnp.dot(left, right, preferred_element_type=F32)


def split(value):
    high = value.astype(BF16)
    return high, (value - high.astype(F32)).astype(BF16)


def spread_kernel(tokens_ref, cotangent_ref, out_ref):
    feats = tokens_ref.shape[1]
    for r in range(out_ref.shape[0]):
        out_ref[r, :, :feats] = tokens_ref[...]
        out_ref[r, :, feats:] = cotangent_ref[...]


def own_table_kernel(base_ref, out_ref):
    for which, sign in ((0, 1.0), (1, -1.0)):
        cos, sin = base_ref[which, 0], base_ref[which, 1]
        span_cos, span_sin = span_table(cos, sin)
        for block in range(out_ref.shape[1] // SPAN):
            at = LOW + MID + block
            c, s = turned(cos[at : at + 1], sin[at : at + 1], span_cos, span_sin)
            rows = slice(block * SPAN, (block + 1) * SPAN)
            out_ref[which, rows, :SPAN] = c.astype(BF16)
            out_ref[which, rows, SPAN:] = (sign * s).astype(BF16)


def late_kernel(rows_ref, cols_ref, coef_ref, after_ref, freq_ref, coef_out):
    del after_ref
    freq_ref[...] = jnp.zeros(freq_ref.shape, jnp.int32)
    coef_out[...] = jnp.zeros(coef_out.shape, F32)
    freq_ref[0:2, :N_COEF] = rows_ref[...]
    freq_ref[2:4, :N_COEF] = cols_ref[...]
    coef_out[:, :N_COEF] = coef_ref[...]


def sum_kernel(*refs):
    total = refs[0][...].astype(F32)
    for ref in refs[1:-1]:
        total += ref[...].astype(F32)
    refs[-1][...] = total.astype(BF16)


def project_kernel(x_ref, table_ref, after_ref, out_ref):
    del after_ref
    feats = x_ref.shape[1] // 2
    for which in range(2):
        values = x_ref[:, which * feats : (which + 1) * feats]
        lanes = slice(2 * which * SPAN, 2 * (which + 1) * SPAN)
        out_ref[:, lanes] = matmul(values, table_ref[which]).astype(BF16)


def first_kernel(
    order_ref, x_ref, gate_ref, up_ref, down_ref, *refs
):
    out_refs, (gates, ups, downs, sems) = refs[:4], refs[4:]
    _, feats, wide = gates.shape
    half = x_ref.shape[0] // 2
    copies = []
    for i in range(gates.shape[0]):
        units = pl.ds(pl.multiple_of(order_ref[i] * wide, SPAN), wide)
        copies.append(
            (
                pltpu.make_async_copy(gate_ref.at[:, units], gates.at[i], sems.at[i, 0]),
                pltpu.make_async_copy(up_ref.at[:, units], ups.at[i], sems.at[i, 1]),
                pltpu.make_async_copy(down_ref.at[units, :], downs.at[i], sems.at[i, 2]),
            )
        )
        for copy in copies[-1]:
            copy.start()
    tokens = x_ref[:, :feats]
    cotangent = x_ref[:, feats:]
    send_a, send_b, keep_a, keep_b = out_refs
    places = (
        ((send_a, 0), (keep_b, 0)),
        ((send_a, 1), (send_b, 0)),
        ((keep_a, 0), (send_b, 1)),
        ((keep_a, 1), (keep_b, 1)),
    )
    for i, (low, high) in enumerate(places):
        for copy in copies[i]:
            copy.wait()
        parts = (
            matmul(tokens, gates[i]),
            matmul(tokens, ups[i]),
            against(cotangent, downs[i]),
        )
        for at, part in enumerate(parts):
            lanes = slice(at * wide, (at + 1) * wide)
            low[0][low[1], :, lanes] = part[:half].astype(BF16)
            high[0][high[1], :, lanes] = part[half:].astype(BF16)


def fold_kernel(keep_a, keep_b, got_a, got_b, send_a, send_b):
    send_a[...] = (keep_a[0].astype(F32) + got_a[0].astype(F32)).astype(BF16)
    send_b[...] = (keep_b[0].astype(F32) + got_b[0].astype(F32)).astype(BF16)


def close_kernel(keep_a, keep_b, got_a, got_b, last_a, last_b, proj_ref, out_ref, proj_out):
    proj_out[...] = proj_ref[...]
    half = last_a.shape[0]
    out_ref[:half] = (
        keep_a[0].astype(F32) + got_a[0].astype(F32) + last_a[...].astype(F32)
    ).astype(BF16)
    out_ref[half:] = (
        keep_b[0].astype(F32) + got_b[0].astype(F32) + last_b[...].astype(F32)
    ).astype(BF16)


def delta_kernel(
    order_ref, down_ref, coef_ref, base_ref, base_out_ref, turn_ref, after_ref, out_ref, *scratch
):
    del after_ref
    left, right, right_turned, down, sems = scratch
    step = pl.program_id(0)
    wide, feats = out_ref.shape
    count = order_ref.shape[0]

    def copy(k):
        units = pl.ds(pl.multiple_of(order_ref[k] * wide, SPAN), wide)
        return pltpu.make_async_copy(down_ref.at[units], down.at[k], sems.at[k])

    @pl.when(step == 0)
    def _():
        for k in range(count):
            copy(k).start()
        for tile in range(PAD // SPAN):
            lanes = slice(tile * SPAN, (tile + 1) * SPAN)
            sines = slice(PAD + tile * SPAN, PAD + (tile + 1) * SPAN)
            cos, sin = base_ref[0, :, lanes], base_ref[1, :, lanes]
            span_cos, span_sin = span_table(cos, sin)
            for block in range(wide // SPAN):
                at = LOW + MID + block
                c, s = turned(cos[at : at + 1], sin[at : at + 1], span_cos, span_sin)
                units = slice(block * SPAN, (block + 1) * SPAN)
                left[units, lanes] = c.astype(BF16)
                left[units, sines] = s.astype(BF16)
            coef = coef_ref[1:2, lanes] * SCALE_DOWN
            cos, sin = base_out_ref[0, :, lanes], base_out_ref[1, :, lanes]
            span_cos, span_sin = span_table(cos, sin)
            for block in range(feats // SPAN):
                at = LOW + MID + block
                c, s = turned(cos[at : at + 1], sin[at : at + 1], span_cos, span_sin)
                rows = slice(block * SPAN, (block + 1) * SPAN)
                right[0, rows, lanes] = c * coef
                right[1, rows, lanes] = -s * coef

    for tile in range(PAD // SPAN):
        lanes = slice(tile * SPAN, (tile + 1) * SPAN)
        sines = slice(PAD + tile * SPAN, PAD + (tile + 1) * SPAN)
        cos, sin = turn_ref[0, 0:1, lanes], turn_ref[0, 1:2, lanes]
        for rows in (slice(i, i + 64) for i in range(0, feats, 64)):
            c, s = right[0, rows, lanes], right[1, rows, lanes]
            right_turned[rows, lanes] = (cos * c + sin * s).astype(BF16)
            right_turned[rows, sines] = (cos * s - sin * c).astype(BF16)
    delta = against(left[...], right_turned[...])
    copy(step).wait()
    out_ref[...] = (down[step].astype(F32) + delta).astype(BF16)


def summed(ref, first, last):
    total = ref[0, :, first:last].astype(F32)
    for z in range(1, ref.shape[0]):
        total += ref[z, :, first:last].astype(F32)
    return total


def twice(ref, row):
    return jnp.concatenate([ref[row : row + 1], ref[row : row + 1]], axis=1)


def middle_kernel(
    source_ref, sums_ref, proj_ref, coef_ref, base_ref, out_ref, span_ref
):
    rows, lanes_sent = out_ref.shape[1:]
    wide = lanes_sent - SPAN
    blocks = wide // SPAN
    for which in range(2):
        for tile in range(PAD // SPAN):
            lanes = slice(tile * SPAN, (tile + 1) * SPAN)
            c, s = span_table(base_ref[which, 0, :, lanes], base_ref[which, 1, :, lanes])
            span_ref[which, :, lanes] = c.astype(BF16)
            span_ref[which, :, PAD + tile * SPAN : PAD + (tile + 1) * SPAN] = s.astype(BF16)

    def phase(which, block):
        at = slice(LOW + MID + block, LOW + MID + block + 1)
        return base_ref[which, 0, at, :], base_ref[which, 1, at, :]

    def spread(weighted, which, sign):
        by_cos, by_sin = weighted[:, :PAD], sign * weighted[:, PAD:]
        pieces = []
        for block in range(blocks):
            cos, sin = phase(which, block)
            pieces.append(
                jnp.concatenate(
                    [by_cos * cos + by_sin * sin, by_sin * cos - by_cos * sin], axis=1
                ).astype(BF16)
            )
        value = against(jnp.concatenate(pieces, axis=0), span_ref[which])
        return jnp.concatenate(
            [value[block * rows : (block + 1) * rows] for block in range(blocks)], axis=1
        )

    def collect(value, which, sign):
        stacked = jnp.concatenate(
            [value[:, block * SPAN : (block + 1) * SPAN] for block in range(blocks)], axis=0
        )
        found = matmul(stacked, span_ref[which])
        by_cos = jnp.zeros((rows, PAD), F32)
        by_sin = jnp.zeros((rows, PAD), F32)
        for block in range(blocks):
            cos, sin = phase(which, block)
            x = found[block * rows : (block + 1) * rows, :PAD]
            y = found[block * rows : (block + 1) * rows, PAD:]
            by_cos += cos * x - sin * y
            by_sin += sin * x + cos * y
        return by_cos, sign * by_sin

    def kind(k):
        lanes = slice(k * SPAN, (k + 1) * SPAN)
        return [
            proj_ref[source_ref[x], source_ref[4 + c], :, lanes].astype(F32)
            for x in range(proj_ref.shape[0])
            for c in range(proj_ref.shape[1])
        ]

    proj_up = jnp.concatenate(kind(0) + kind(1), axis=1)
    back_down = jnp.concatenate(kind(2) + kind(3), axis=1)
    gate = summed(sums_ref, 0, wide)
    up = summed(sums_ref, wide, 2 * wide) + spread(proj_up * (twice(coef_ref, 0) * SCALE_UP), 0, -1.0)
    dhidden = summed(sums_ref, 2 * wide, 3 * wide) + spread(back_down * (twice(coef_ref, 1) * SCALE_DOWN), 1, 1.0)
    activated = (gate / (1.0 + jnp.exp(-gate))).astype(BF16).astype(F32)
    hidden = (activated * up).astype(BF16)
    dup = (dhidden * activated).astype(BF16)
    up_cos, up_sin = collect(dup, 0, -1.0)
    down_cos, down_sin = collect(hidden, 1, 1.0)

    def over_tokens(value):
        return jnp.sum(value, axis=0, keepdims=True)

    grad_up = SCALE_UP * over_tokens(proj_up[:, :PAD] * up_cos + proj_up[:, PAD:] * up_sin)
    grad_down = SCALE_DOWN * over_tokens(
        down_cos * back_down[:, :PAD] + down_sin * back_down[:, PAD:]
    )
    grads = jnp.concatenate(
        [g[:, k * SPAN : (k + 1) * SPAN] for g in (grad_up, grad_down) for k in range(PAD // SPAN)],
        axis=0,
    ).astype(BF16)
    for c in range(out_ref.shape[0]):
        out_ref[c, :, :wide] = hidden
        out_ref[c, :, wide:] = grads


def regroup_kernel(in_ref, out_ref):
    peers, rows, _ = in_ref.shape
    wide = out_ref.shape[1]
    grads = jnp.zeros((rows, SPAN), F32)
    for z in range(peers):
        out_ref[z * rows : (z + 1) * rows, :] = in_ref[z, :, :wide]
        grads += in_ref[z, :, wide:].astype(F32)
    high, low = split(grads)
    out_ref[peers * rows :, :SPAN] = high
    out_ref[peers * rows :, SPAN : 2 * SPAN] = low
    out_ref[peers * rows :, 2 * SPAN :] = jnp.zeros((rows, wide - 2 * SPAN), BF16)


def last_kernel(own_ref, one_ref, two_ref, three_ref, weight_ref, out_ref):
    peers, rows, feats = out_ref.shape
    rows //= 2
    wide = own_ref.shape[1]
    count = peers * rows
    total = jnp.zeros((count, feats), F32)
    grads = jnp.zeros((own_ref.shape[0] - count, SPAN), F32)
    for k, ref in enumerate((own_ref, one_ref, two_ref, three_ref)):
        units = slice(k * wide, (k + 1) * wide)
        total += matmul(ref[:count, :], weight_ref[units, :])
        grads += ref[count:, :SPAN].astype(F32) + ref[count:, SPAN : 2 * SPAN].astype(F32)
    high, low = split(grads)
    for r in range(peers):
        out_ref[r, :rows, :] = total[r * rows : (r + 1) * rows, :].astype(BF16)
        out_ref[r, rows:, :SPAN] = high
        out_ref[r, rows:, SPAN:] = low


def update_kernel(in_ref, first_ref, second_ref, mixed_ref, step_ref, scratch):
    peers, rows, _ = in_ref.shape
    rows //= 2
    mixed = jnp.zeros(mixed_ref.shape, F32)
    pieces = jnp.zeros((rows, SPAN), F32)
    for r in range(peers):
        mixed += in_ref[r, :rows, :].astype(F32)
        pieces += in_ref[r, rows:, :SPAN].astype(F32)
        pieces += in_ref[r, rows:, SPAN:].astype(F32)
    mixed_ref[...] = mixed.astype(BF16)
    per = PAD // SPAN
    for k in range(rows):
        at = k % per
        scratch[k // per : k // per + 1, at * SPAN : (at + 1) * SPAN] = pieces[k : k + 1]
    grads = scratch[:, :N_COEF]
    squares = jnp.sum(jnp.sum(grads * grads, axis=1, keepdims=True), axis=0, keepdims=True)
    norm_value = jnp.sqrt(squares)
    clipped = grads * jnp.minimum(1.0, 1.0 / (norm_value + 1e-06))
    first = 0.9 * first_ref[...] + 0.1 * clipped
    second = 0.999 * second_ref[...] + 0.001 * clipped * clipped
    step_ref[...] = (
        first / (1.0 - 0.9**ADAM_STEP) / (jnp.sqrt(second / (1.0 - 0.999**ADAM_STEP)) + 1e-08)
    )


def on_device(
    tokens,
    cotangent,
    gate_weight,
    up_weight,
    down_weight,
    coefficients,
    spectral_rows,
    spectral_cols,
    adam_first,
    adam_second,
):
    peers_row = lax.axis_size(PLANE)
    peers_z = lax.axis_size("z")
    peers_y = lax.axis_size("y")
    row_index = lax.axis_index(PLANE)
    z_index = lax.axis_index("z")
    y_index = lax.axis_index("y")
    own, feats = tokens.shape
    units = gate_weight.shape[1]
    wide = units // peers_y
    count = own * peers_row
    feat_first = (z_index * peers_y + y_index) * feats
    unit_first = row_index * units

    def exchange(value, axes):
        return lax.all_to_all(value, axes, 0, 0, tiled=True)

    def padded(values):
        return jnp.pad(values, (0, PAD - N_COEF))

    lanes = row_index * SPAN
    own_left = lax.dynamic_slice_in_dim(padded(spectral_rows[0]), lanes, SPAN)
    own_right = lax.dynamic_slice_in_dim(padded(spectral_cols[1]), lanes, SPAN)
    base_own = jnp.stack(
        [
            phases(own_left, feat_first, feats // SPAN, D),
            phases(own_right, feat_first, feats // SPAN, D),
        ]
    )

    both = pl.pallas_call(
        spread_kernel,
        in_specs=[VMEM] * 2,
        out_specs=VMEM,
        out_shape=jax.ShapeDtypeStruct((peers_row, own, 2 * feats), BF16),
    )(tokens, cotangent)
    both = exchange(both, PLANE).reshape(count, 2 * feats)

    share = count // peers_z
    half = count // 2
    block = 3 * wide
    smem = pl.BlockSpec(memory_space=pltpu.SMEM)
    hbm = pl.BlockSpec(memory_space=pltpu.HBM)
    anywhere = pl.BlockSpec(memory_space=pl.ANY)
    order = y_index ^ jnp.array([1, 2, 3, 0], jnp.int32)
    pieces = jax.ShapeDtypeStruct((2, half, block), BF16)

    def full(shape):
        return pl.BlockSpec(shape, lambda i: (0,) * len(shape))

    table = pl.pallas_call(
        own_table_kernel,
        in_specs=[VMEM],
        out_specs=VMEM,
        out_shape=jax.ShapeDtypeStruct((2, feats, 2 * SPAN), BF16),
        compiler_params=params(8),
    )(base_own)
    send_a, send_b, keep_a, keep_b = pl.pallas_call(
        first_kernel,
        in_specs=[smem, VMEM, hbm, hbm, hbm],
        out_specs=[VMEM] * 4,
        out_shape=[pieces] * 4,
        scratch_shapes=[
            pltpu.VMEM((peers_y, feats, wide), BF16),
            pltpu.VMEM((peers_y, feats, wide), BF16),
            pltpu.VMEM((peers_y, wide, feats), BF16),
            pltpu.SemaphoreType.DMA((peers_y, 3)),
        ],
        compiler_params=params(60),
    )(order, both, gate_weight, up_weight, down_weight)

    def swap(value, mask):
        return lax.ppermute(value, "y", [(y, y ^ mask) for y in range(peers_y)])

    got_a, got_b = swap(send_a, 1), swap(send_b, 3)
    proj = pl.pallas_call(
        project_kernel,
        in_specs=[VMEM] * 2 + [anywhere],
        out_specs=VMEM,
        out_shape=jax.ShapeDtypeStruct((count, peers_y * SPAN), BF16),
        compiler_params=params(8),
    )(both, table, keep_a)
    proj = exchange(proj.reshape(peers_z, share, peers_y * SPAN), "z")

    freq, coefs = pl.pallas_call(
        late_kernel,
        in_specs=[VMEM] * 3 + [anywhere],
        out_specs=[VMEM] * 2,
        out_shape=[
            jax.ShapeDtypeStruct((4, PAD), jnp.int32),
            jax.ShapeDtypeStruct((2, PAD), F32),
        ],
    )(spectral_rows, spectral_cols, coefficients, keep_a)
    tile_first = unit_first + y_index * wide
    base_up = phases(freq[2], tile_first, wide // SPAN, FF)
    base_down = phases(freq[1], tile_first, wide // SPAN, FF)
    base_out = phases(freq[3], feat_first, feats // SPAN, D)
    sources = (y_index - jnp.arange(peers_y, dtype=jnp.int32)) & 3
    turns = waves(((sources - y_index) * wide)[:, None], freq[1], FF, 1)
    turns = turns.reshape(peers_y, 2, PAD)

    def added(values):
        return pl.pallas_call(
            sum_kernel,
            in_specs=[VMEM] * len(values),
            out_specs=VMEM,
            out_shape=jax.ShapeDtypeStruct(values[0].shape, BF16),
            compiler_params=params(8),
        )(*values)

    def turn(value, axis, peers, k):
        return lax.ppermute(value, axis, [(i, (i + k) % peers) for i in range(peers)])

    proj = jnp.sum(proj.astype(F32), axis=0).astype(BF16)
    proj = added([proj] + [turn(proj, "y", peers_y, k) for k in (1, 2, 3)])
    def whole(rows):
        return pl.BlockSpec((1, half, block), lambda i: (rows, 0, 0))

    send_a, send_b = pl.pallas_call(
        fold_kernel,
        grid=(1,),
        in_specs=[whole(0), whole(0), whole(1), whole(0)],
        out_specs=[full((half, block))] * 2,
        out_shape=[jax.ShapeDtypeStruct((half, block), BF16)] * 2,
        compiler_params=params(12),
    )(keep_a, keep_b, got_a, got_b)
    last_a, last_b = swap(send_a, 3), swap(send_b, 1)
    sums, proj = pl.pallas_call(
        close_kernel,
        grid=(1,),
        in_specs=[whole(1), whole(1), whole(0), whole(1)] + [full((half, block))] * 2
        + [full(proj.shape)],
        out_specs=[full((count, block)), full(proj.shape)],
        out_shape=[
            jax.ShapeDtypeStruct((count, block), BF16),
            jax.ShapeDtypeStruct(proj.shape, BF16),
        ],
        compiler_params=params(12),
    )(keep_a, keep_b, got_a, got_b, last_a, last_b, proj)
    proj = jnp.stack([proj, lax.ppermute(proj, "core", [(0, 1), (1, 0)])])
    proj = jnp.stack([proj] + [turn(proj, "x", 4, k) for k in (1, 2, 3)])
    chip = (lax.axis_index("x") - jnp.arange(4, dtype=jnp.int32)) & 3
    core = lax.axis_index("core") ^ jnp.arange(2, dtype=jnp.int32)
    source = jnp.concatenate([chip, core])
    sums = exchange(sums.reshape(peers_z, share, block), "z")

    hidden = pl.pallas_call(
        middle_kernel,
        in_specs=[smem] + [VMEM] * 4,
        out_specs=VMEM,
        out_shape=jax.ShapeDtypeStruct((peers_z, share, wide + SPAN), BF16),
        scratch_shapes=[pltpu.VMEM((2, SPAN, 2 * PAD), BF16)],
        compiler_params=params(12),
    )(source, sums, proj, coefs, jnp.stack([base_up, base_down]))
    hidden = exchange(hidden, "z")
    hidden = pl.pallas_call(
        regroup_kernel,
        in_specs=[VMEM],
        out_specs=VMEM,
        out_shape=jax.ShapeDtypeStruct((count + share, wide), BF16),
        compiler_params=params(8),
    )(hidden)
    weight = pl.pallas_call(
        delta_kernel,
        grid=(peers_y,),
        in_specs=[
            smem,
            hbm,
            full(coefs.shape),
            full(base_down.shape),
            full(base_out.shape),
            pl.BlockSpec((1,) + turns.shape[1:], lambda i: (i, 0, 0)),
            anywhere,
        ],
        out_specs=pl.BlockSpec((wide, feats), lambda i: (i, 0)),
        out_shape=jax.ShapeDtypeStruct((units, feats), BF16),
        scratch_shapes=[
            pltpu.VMEM((wide, 2 * PAD), BF16),
            pltpu.VMEM((2, feats, PAD), F32),
            pltpu.VMEM((feats, 2 * PAD), BF16),
            pltpu.VMEM((peers_y, wide, feats), BF16),
            pltpu.SemaphoreType.DMA((peers_y,)),
        ],
        compiler_params=params(20),
        cost_estimate=pl.CostEstimate(
            flops=6 << 30, bytes_accessed=8 << 20, transcendentals=0
        ),
    )(sources, down_weight, coefs, base_down, base_out, turns, hidden)

    def shifted(k):
        return lax.ppermute(hidden, "y", [(y, (y + k) % peers_y) for y in range(peers_y)])

    others = [shifted(1), shifted(2), shifted(3)]
    mixed = pl.pallas_call(
        last_kernel,
        in_specs=[VMEM] * 5,
        out_specs=VMEM,
        out_shape=jax.ShapeDtypeStruct((peers_row, 2 * own, feats), BF16),
        compiler_params=params(12),
    )(hidden, *others, weight)
    mixed = exchange(mixed, PLANE)

    return pl.pallas_call(
        update_kernel,
        in_specs=[VMEM] * 3,
        out_specs=[VMEM] * 2,
        out_shape=[
            jax.ShapeDtypeStruct((own, feats), BF16),
            jax.ShapeDtypeStruct(adam_first.shape, F32),
        ],
        scratch_shapes=[pltpu.VMEM((2, PAD), F32)],
    )(mixed, adam_first, adam_second)


def solution(mesh):
    chips = Mesh(mesh.devices.reshape(4, 2, 8, 4), ("x", "core", "z", "y"))
    tiles = P(("x", "core"), ("z", "y"))
    weights = P(("z", "y"), ("x", "core"))
    placed = (tiles, tiles, weights, weights, tiles, P(), P(), P(), P(), P())
    return jax.shard_map(
        on_device, mesh=chips, in_specs=placed, out_specs=(tiles, P()), check_vma=False
    )
```

profile of v0, /device:TPU:1, one launch (start us, length us, event | category | flops | bytes accessed | tf_op | source)
XLA Modules:
  0.0 120.6 jit_solution(10109384085934950810)
XLA Ops:
  0.6 1.4 %shard_map.122 = bf16[8,16,512]{2,1,0:T(8,128)(2,1)} custom-call(bf16[16,256]{1,0:T(8,128)(2,1)} %tokens_ref.1, bf16[16,256]{1,0:T(8,128)(2,1)} %cotangent_ref.1), custom_call_target="tpu_custom_call" | custom-call | tf_op jit(solution)/shard_map/pallas_call | solution.py:424
  2.0 6.5 %all-to-all-start = ((bf16[8,16,512]{2,1,0:T(8,128)(2,1)}), bf16[8,16,512]{2,1,0:T(8,128)(2,1)S(1)}, u32[]{:S(2)}, u32[]{:S(2)}) async-start(bf16[8,16,512]{2,1,0:T(8,128)(2,1)} %shard_map.122), calls=%async_computation | async-start | bytes 262144 | tf_op jit(solution)/shard_map/all_to_all | solution.py:409
  11.3 2.5 %all-to-all-done = bf16[8,16,512]{2,1,0:T(8,128)(2,1)S(1)} async-done(((bf16[8,16,512]{2,1,0:T(8,128)(2,1)}), bf16[8,16,512]{2,1,0:T(8,128)(2,1)S(1)}, u32[]{:S(2)}, u32[]{:S(2)}) %all-to-all-start) | async-done | bytes 131104 | tf_op jit(solution)/shard_map/all_to_all | solution.py:409
  14.5 5.3 %shard_map.123 = (bf16[2,64,2688]{2,1,0:T(8,128)(2,1)}, bf16[2,64,2688]{2,1,0:T(8,128)(2,1)}, bf16[2,64,2688]{2,1,0:T(8,128)(2,1)}, bf16[2,64,2688]{2,1,0:T(8,128)(2,1)}) custom-call(s32[4]{0:T(128)} %broadcast_xor_fusion.order_ref, bf16[128,512]{1,0:T(8,128)(2,1)} %bitcast.25, bf16[256,3584]{1,0:T(8,128)(2,1)} %gate_ref.1, bf16[256,3584]{1,0:T(8,128)(2,1)} %up_ref.1, ...), custom_call_target="tpu_custom_call" | custom-call | tf_op jit(solution)/shard_map/pallas_call | solution.py:451
  20.4 1.9 %collective-permute-start.1 = (bf16[2,64,2688]{2,1,0:T(8,128)(2,1)}, bf16[2,64,2688]{2,1,0:T(8,128)(2,1)S(1)}, u32[]{:S(2)}, u32[]{:S(2)}) collective-permute-start(bf16[2,64,2688]{2,1,0:T(8,128)(2,1)} %get-tuple-element.15), channel_id=1, source_target_pairs={{0,3},{1,2},{2,1},{3,0},{4,7},{5,6},{6,5},{7,4},{8,11},{9,10},{10,... | collective-permute-start | bytes 2064392 | tf_op jit(solution)/shard_map/ppermute | solution.py:466
  25.6 8.2 %all-to-all-start.1 = ((bf16[8,16,512]{2,1,0:T(8,128)(2,1)}), bf16[8,16,512]{2,1,0:T(8,128)(2,1)}, u32[]{:S(2)}, u32[]{:S(2)}) async-start(bf16[8,16,512]{2,1,0:T(8,128)(2,1)} %bitcast.5), calls=%async_computation.1 | async-start | bytes 262144 | tf_op jit(solution)/shard_map/all_to_all | solution.py:409
  33.8 2.4 %collective-permute-done.got_a = bf16[2,64,2688]{2,1,0:T(8,128)(2,1)S(1)} collective-permute-done((bf16[2,64,2688]{2,1,0:T(8,128)(2,1)}, bf16[2,64,2688]{2,1,0:T(8,128)(2,1)S(1)}, u32[]{:S(2)}, u32[]{:S(2)}) %collective-permute-start) | collective-permute-done | bytes 688160 | tf_op jit(solution)/shard_map/ppermute | solution.py:466
  36.1 1.5 %collective-permute-done.1.got_b = bf16[2,64,2688]{2,1,0:T(8,128)(2,1)S(1)} collective-permute-done((bf16[2,64,2688]{2,1,0:T(8,128)(2,1)}, bf16[2,64,2688]{2,1,0:T(8,128)(2,1)S(1)}, u32[]{:S(2)}, u32[]{:S(2)}) %collective-permute-start.1) | collective-permute-done | bytes 688160 | tf_op jit(solution)/shard_map/ppermute | solution.py:466
  38.6 1.9 %collective-permute-start.2 = (bf16[64,2688]{1,0:T(8,128)(2,1)}, bf16[64,2688]{1,0:T(8,128)(2,1)S(1)}, u32[]{:S(2)}, u32[]{:S(2)}) collective-permute-start(bf16[64,2688]{1,0:T(8,128)(2,1)} %get-tuple-element.16), channel_id=1, source_target_pairs={{0,3},{1,2},{2,1},{3,0},{4,7},{5,6},{6,5},{7,4},{8,11},{9,10},{10,... | collective-permute-start | bytes 1032200 | tf_op jit(solution)/shard_map/ppermute | solution.py:466
  40.6 1.3 %shard_map.129 = (s32[4,1024]{1,0:T(4,128)}, f32[2,1024]{1,0:T(2,128)}) custom-call(s32[2,1000]{1,0:T(2,128)} %rows_ref.1, s32[2,1000]{1,0:T(2,128)} %cols_ref.1, f32[2,1000]{1,0:T(2,128)} %coef_ref.1, bf16[2,64,2688]{2,1,0:T(8,128)(2,1)} %get-tuple-element.12.keep_a.after_ref), custom_call_target="tpu_custom_call" | custom-call | tf_op jit(solution)/shard_map/pallas_call | solution.py:478
  42.9 1.5 %collective-permute-start.4 = (bf16[16,512]{1,0:T(8,128)(2,1)S(1)}, bf16[16,512]{1,0:T(8,128)(2,1)S(1)}, u32[]{:S(2)}, u32[]{:S(2)}) collective-permute-start(bf16[16,512]{1,0:T(8,128)(2,1)S(1)} %reduce_sum.12.refs_0_), channel_id=1, source_target_pairs={{0,1},{1,2},{2,3},{3,0},{4,5},{5,6},{6,7},{7,4},{8,9},{9,10},{10,1... | collective-permute-start | bytes 49160 | tf_op jit(solution)/shard_map/ppermute | solution.py:505
  45.0 2.0 %collective-permute-start.6 = (bf16[16,512]{1,0:T(8,128)(2,1)S(1)}, bf16[16,512]{1,0:T(8,128)(2,1)S(1)}, u32[]{:S(2)}, u32[]{:S(2)}) collective-permute-start(bf16[16,512]{1,0:T(8,128)(2,1)S(1)} %reduce_sum.12.refs_0_), channel_id=1, source_target_pairs={{0,3},{1,0},{2,1},{3,2},{4,7},{5,4},{6,5},{7,6},{8,11},{9,8},{10,9... | collective-permute-start | bytes 49160 | tf_op jit(solution)/shard_map/ppermute | solution.py:505
  50.0 8.2 %all-to-all-start.2 = ((bf16[8,16,2688]{2,1,0:T(8,128)(2,1)}), bf16[8,16,2688]{2,1,0:T(8,128)(2,1)S(1)}, u32[]{:S(2)}, u32[]{:S(2)}) async-start(bf16[8,16,2688]{2,1,0:T(8,128)(2,1)} %bitcast.6), calls=%async_computation.2 | async-start | bytes 1376256 | tf_op jit(solution)/shard_map/all_to_all | solution.py:409
  60.0 4.1 %collective-permute-start.7 = (bf16[16,512]{1,0:T(8,128)(2,1)S(1)}, bf16[16,512]{1,0:T(8,128)(2,1)S(1)}, u32[]{:S(2)}, u32[]{:S(2)}) collective-permute-start(bf16[16,512]{1,0:T(8,128)(2,1)S(1)} %get-tuple-element.19), channel_id=1, source_target_pairs={{0,32},{32,0},{1,33},{33,1},{2,34},{34,2},{3,35},{35,3},{4,36},{36... | collective-permute-start | bytes 49160 | tf_op jit(solution)/shard_map/ppermute | solution.py:533
  65.8 1.2 collective-permute-start.9
  68.0 2.4 %collective-permute-done.9 = bf16[2,16,512]{2,1,0:T(8,128)(2,1)S(1)} collective-permute-done((bf16[2,16,512]{2,1,0:T(8,128)(2,1)S(1)}, bf16[2,16,512]{2,1,0:T(8,128)(2,1)S(1)}, u32[]{:S(2)}, u32[]{:S(2)}) %collective-permute-start.9) | collective-permute-done | bytes 32800 | tf_op jit(solution)/shard_map/ppermute | solution.py:505
  71.5 5.2 %all-to-all-done.2.sums_ref = bf16[8,16,2688]{2,1,0:T(8,128)(2,1)S(1)} async-done(((bf16[8,16,2688]{2,1,0:T(8,128)(2,1)}), bf16[8,16,2688]{2,1,0:T(8,128)(2,1)S(1)}, u32[]{:S(2)}, u32[]{:S(2)}) %all-to-all-start.2) | async-done | bytes 688160 | tf_op jit(solution)/shard_map/all_to_all | solution.py:409
  76.7 2.7 %shard_map.130 = bf16[8,16,1024]{2,1,0:T(8,128)(2,1)} custom-call(s32[6]{0:T(128)S(1)} %pad_add_fusion.source_ref, bf16[8,16,2688]{2,1,0:T(8,128)(2,1)S(1)} %all-to-all-done.2.sums_ref, bf16[4,2,16,512]{3,2,1,0:T(8,128)(2,1)S(1)} %pad_maximum_fusion.3.proj_ref, f32[2,1024]{1,0:T(2,128)S(1)} %copy-done.7, f32[2,2,32,1024]{3,2,1,0:T(8,128)S(1)} %pad_maximum_fusion.base_ref), custom_call_target="tpu_custom_call" | custom-call | tf_op jit(solution)/shard_map/pallas_call | solution.py:540
  79.4 3.4 %all-to-all-start.3 = ((bf16[8,16,1024]{2,1,0:T(8,128)(2,1)}), bf16[8,16,1024]{2,1,0:T(8,128)(2,1)S(1)}, u32[]{:S(2)}, u32[]{:S(2)}) async-start(bf16[8,16,1024]{2,1,0:T(8,128)(2,1)} %shard_map.130), calls=%async_computation.3 | async-start | bytes 524288 | tf_op jit(solution)/shard_map/all_to_all | solution.py:409
  83.5 8.7 %all-to-all-done.3.in_ref = bf16[8,16,1024]{2,1,0:T(8,128)(2,1)S(1)} async-done(((bf16[8,16,1024]{2,1,0:T(8,128)(2,1)}), bf16[8,16,1024]{2,1,0:T(8,128)(2,1)S(1)}, u32[]{:S(2)}, u32[]{:S(2)}) %all-to-all-start.3) | async-done | bytes 262176 | tf_op jit(solution)/shard_map/all_to_all | solution.py:409
  92.8 3.2 %collective-permute-start.12 = (bf16[144,896]{1,0:T(8,128)(2,1)S(1)}, bf16[144,896]{1,0:T(8,128)(2,1)S(1)}, u32[]{:S(2)}, u32[]{:S(2)}) collective-permute-start(bf16[144,896]{1,0:T(8,128)(2,1)S(1)} %shard_map.131.after_ref.own_ref), channel_id=1, source_target_pairs={{0,2},{1,3},{2,0},{3,1},{4,6},{5,7},{6,4},{7,5},{8,10},{9,11},{10,... | collective-permute-start | bytes 774152 | tf_op jit(solution)/shard_map/ppermute | solution.py:584
  96.1 8.7 %shard_map.132.weight_ref = bf16[3584,256]{1,0:T(8,128)(2,1)S(1)} custom-call(s32[4]{0:T(128)S(1)} %subtract_and_fusion.order_ref, bf16[3584,256]{1,0:T(8,128)(2,1)S(1)} %copy-done.4, f32[2,1024]{1,0:T(2,128)S(1)} %copy-done.7, f32[2,32,1024]{2,1,0:T(8,128)S(1)} %get-tuple-element.22.base_ref, f32[2,32,1024]{2,1,0:T(8,128)S(1)} %pad_maximum_fusion.2.base_out_ref, ...), custom_call_target="tpu_custom_call" | custom-call | flops 6442450944 | bytes 8388608 | tf_op jit(solution)/shard_map/pallas_call | solution.py:556
  105.3 13.7 %all_to_all.25.in_ref = bf16[8,32,256]{2,1,0:T(8,128)(2,1)} all-to-all(bf16[8,32,256]{2,1,0:T(8,128)(2,1)S(1)} %shard_map.133), channel_id=1, replica_groups=mesh['x'=4,'core'=2,'z'=8,'y'=4] {'x','core'}, dimensions={0} | all-to-all | bytes 262144 | tf_op jit(solution)/shard_map/all_to_all | solution.py:409
  118.9 1.7 %shard_map.134 = (bf16[16,256]{1,0:T(8,128)(2,1)}, f32[2,1000]{1,0:T(2,128)}) custom-call(bf16[8,32,256]{2,1,0:T(8,128)(2,1)} %all_to_all.25.in_ref, f32[2,1000]{1,0:T(2,128)} %first_ref.1, f32[2,1000]{1,0:T(2,128)} %second_ref.1), custom_call_target="tpu_custom_call" | custom-call | tf_op jit(solution)/shard_map/pallas_call | solution.py:596
  (74 shorter events, 20.3 us)
Async XLA Ops:
  2.0 11.8 %all-to-all-start = ((bf16[8,16,512]{2,1,0:T(8,128)(2,1)}), bf16[8,16,512]{2,1,0:T(8,128)(2,1)S(1)}, u32[]{:S(2)}, u32[]{:S(2)}) async-start(bf16[8,16,512]{2,1,0:T(8,128)(2,1)} %shard_map.122), calls=%async_computation | async-start | bytes 262144 | tf_op jit(solution)/shard_map/all_to_all | solution.py:409
  19.8 16.4 %collective-permute-start = (bf16[2,64,2688]{2,1,0:T(8,128)(2,1)}, bf16[2,64,2688]{2,1,0:T(8,128)(2,1)S(1)}, u32[]{:S(2)}, u32[]{:S(2)}) collective-permute-start(bf16[2,64,2688]{2,1,0:T(8,128)(2,1)} %get-tuple-element.14), channel_id=1, source_target_pairs={{0,1},{1,0},{2,3},{3,2},{4,5},{5,4},{6,7},{7,6},{8,9},{9,8},{10,11... | collective-permute-start | bytes 2064392 | tf_op jit(solution)/shard_map/ppermute | solution.py:466
  20.4 17.2 %collective-permute-start.1 = (bf16[2,64,2688]{2,1,0:T(8,128)(2,1)}, bf16[2,64,2688]{2,1,0:T(8,128)(2,1)S(1)}, u32[]{:S(2)}, u32[]{:S(2)}) collective-permute-start(bf16[2,64,2688]{2,1,0:T(8,128)(2,1)} %get-tuple-element.15), channel_id=1, source_target_pairs={{0,3},{1,2},{2,1},{3,0},{4,7},{5,6},{6,5},{7,4},{8,11},{9,10},{10,... | collective-permute-start | bytes 2064392 | tf_op jit(solution)/shard_map/ppermute | solution.py:466
  22.7 1.1 copy-start
  24.7 12.9 %copy-start.1 = (bf16[2,64,2688]{2,1,0:T(8,128)(2,1)S(1)}, bf16[2,64,2688]{2,1,0:T(8,128)(2,1)}, u32[]{:S(2)}) copy-start(bf16[2,64,2688]{2,1,0:T(8,128)(2,1)} %get-tuple-element.12.keep_a.after_ref) | copy-start | bytes 2064388
  24.7 12.9 %copy-start.3 = (bf16[2,64,2688]{2,1,0:T(8,128)(2,1)S(1)}, bf16[2,64,2688]{2,1,0:T(8,128)(2,1)}, u32[]{:S(2)}) copy-start(bf16[2,64,2688]{2,1,0:T(8,128)(2,1)} %get-tuple-element.13.keep_b) | copy-start | bytes 2064388
  25.6 16.4 %all-to-all-start.1 = ((bf16[8,16,512]{2,1,0:T(8,128)(2,1)}), bf16[8,16,512]{2,1,0:T(8,128)(2,1)}, u32[]{:S(2)}, u32[]{:S(2)}) async-start(bf16[8,16,512]{2,1,0:T(8,128)(2,1)} %bitcast.5), calls=%async_computation.1 | async-start | bytes 262144 | tf_op jit(solution)/shard_map/all_to_all | solution.py:409
  37.6 11.2 %copy-start.2 = (bf16[2,64,2688]{2,1,0:T(8,128)(2,1)S(1)}, bf16[2,64,2688]{2,1,0:T(8,128)(2,1)}, u32[]{:S(2)}) copy-start(bf16[2,64,2688]{2,1,0:T(8,128)(2,1)} %get-tuple-element.12.keep_a.after_ref) | copy-start | bytes 2064388
  38.6 10.2 %collective-permute-start.2 = (bf16[64,2688]{1,0:T(8,128)(2,1)}, bf16[64,2688]{1,0:T(8,128)(2,1)S(1)}, u32[]{:S(2)}, u32[]{:S(2)}) collective-permute-start(bf16[64,2688]{1,0:T(8,128)(2,1)} %get-tuple-element.16), channel_id=1, source_target_pairs={{0,3},{1,2},{2,1},{3,0},{4,7},{5,6},{6,5},{7,4},{8,11},{9,10},{10,... | collective-permute-start | bytes 1032200 | tf_op jit(solution)/shard_map/ppermute | solution.py:466
  40.5 8.4 %collective-permute-start.3 = (bf16[64,2688]{1,0:T(8,128)(2,1)}, bf16[64,2688]{1,0:T(8,128)(2,1)S(1)}, u32[]{:S(2)}, u32[]{:S(2)}) collective-permute-start(bf16[64,2688]{1,0:T(8,128)(2,1)} %get-tuple-element.17), channel_id=1, source_target_pairs={{0,1},{1,0},{2,3},{3,2},{4,5},{5,4},{6,7},{7,6},{8,9},{9,8},{10,11... | collective-permute-start | bytes 1032200 | tf_op jit(solution)/shard_map/ppermute | solution.py:466
  42.9 5.0 %collective-permute-start.4 = (bf16[16,512]{1,0:T(8,128)(2,1)S(1)}, bf16[16,512]{1,0:T(8,128)(2,1)S(1)}, u32[]{:S(2)}, u32[]{:S(2)}) collective-permute-start(bf16[16,512]{1,0:T(8,128)(2,1)S(1)} %reduce_sum.12.refs_0_), channel_id=1, source_target_pairs={{0,1},{1,2},{2,3},{3,0},{4,5},{5,6},{6,7},{7,4},{8,9},{9,10},{10,1... | collective-permute-start | bytes 49160 | tf_op jit(solution)/shard_map/ppermute | solution.py:505
  44.4 4.4 %collective-permute-start.5 = (bf16[16,512]{1,0:T(8,128)(2,1)S(1)}, bf16[16,512]{1,0:T(8,128)(2,1)S(1)}, u32[]{:S(2)}, u32[]{:S(2)}) collective-permute-start(bf16[16,512]{1,0:T(8,128)(2,1)S(1)} %reduce_sum.12.refs_0_), channel_id=1, source_target_pairs={{0,2},{1,3},{2,0},{3,1},{4,6},{5,7},{6,4},{7,5},{8,10},{9,11},{10,... | collective-permute-start | bytes 49160 | tf_op jit(solution)/shard_map/ppermute | solution.py:505
  45.0 3.8 %collective-permute-start.6 = (bf16[16,512]{1,0:T(8,128)(2,1)S(1)}, bf16[16,512]{1,0:T(8,128)(2,1)S(1)}, u32[]{:S(2)}, u32[]{:S(2)}) collective-permute-start(bf16[16,512]{1,0:T(8,128)(2,1)S(1)} %reduce_sum.12.refs_0_), channel_id=1, source_target_pairs={{0,3},{1,0},{2,1},{3,2},{4,7},{5,4},{6,5},{7,6},{8,11},{9,8},{10,9... | collective-permute-start | bytes 49160 | tf_op jit(solution)/shard_map/ppermute | solution.py:505
  50.0 26.7 %all-to-all-start.2 = ((bf16[8,16,2688]{2,1,0:T(8,128)(2,1)}), bf16[8,16,2688]{2,1,0:T(8,128)(2,1)S(1)}, u32[]{:S(2)}, u32[]{:S(2)}) async-start(bf16[8,16,2688]{2,1,0:T(8,128)(2,1)} %bitcast.6), calls=%async_computation.2 | async-start | bytes 1376256 | tf_op jit(solution)/shard_map/all_to_all | solution.py:409
  58.2 18.5 %copy-start.7 = (f32[2,1024]{1,0:T(2,128)S(1)}, f32[2,1024]{1,0:T(2,128)}, u32[]{:S(2)}) copy-start(f32[2,1024]{1,0:T(2,128)} %get-tuple-element.20.coef_ref) | copy-start | bytes 24580
  60.0 5.0 %collective-permute-start.7 = (bf16[16,512]{1,0:T(8,128)(2,1)S(1)}, bf16[16,512]{1,0:T(8,128)(2,1)S(1)}, u32[]{:S(2)}, u32[]{:S(2)}) collective-permute-start(bf16[16,512]{1,0:T(8,128)(2,1)S(1)} %get-tuple-element.19), channel_id=1, source_target_pairs={{0,32},{32,0},{1,33},{33,1},{2,34},{34,2},{3,35},{35,3},{4,36},{36... | collective-permute-start | bytes 49160 | tf_op jit(solution)/shard_map/ppermute | solution.py:533
  64.9 3.1 %collective-permute-start.10 = (bf16[2,16,512]{2,1,0:T(8,128)(2,1)S(1)}, bf16[2,16,512]{2,1,0:T(8,128)(2,1)S(1)}, u32[]{:S(2)}, u32[]{:S(2)}) collective-permute-start(bf16[2,16,512]{2,1,0:T(8,128)(2,1)S(1)} %get-tuple-element.25), channel_id=1, source_target_pairs={{0,192},{64,0},{128,64},{192,128},{1,193},{65,1},{129,65},{193,129... | collective-permute-start | bytes 98312 | tf_op jit(solution)/shard_map/ppermute | solution.py:505
  65.8 4.6 %collective-permute-start.9 = (bf16[2,16,512]{2,1,0:T(8,128)(2,1)S(1)}, bf16[2,16,512]{2,1,0:T(8,128)(2,1)S(1)}, u32[]{:S(2)}, u32[]{:S(2)}) collective-permute-start(bf16[2,16,512]{2,1,0:T(8,128)(2,1)S(1)} %get-tuple-element.25), channel_id=1, source_target_pairs={{0,128},{64,192},{128,0},{192,64},{1,129},{65,193},{129,1},{193,65... | collective-permute-start | bytes 98312 | tf_op jit(solution)/shard_map/ppermute | solution.py:505
  67.0 4.5 %collective-permute-start.8 = (bf16[2,16,512]{2,1,0:T(8,128)(2,1)S(1)}, bf16[2,16,512]{2,1,0:T(8,128)(2,1)S(1)}, u32[]{:S(2)}, u32[]{:S(2)}) collective-permute-start(bf16[2,16,512]{2,1,0:T(8,128)(2,1)S(1)} %get-tuple-element.25), channel_id=1, source_target_pairs={{0,64},{64,128},{128,192},{192,0},{1,65},{65,129},{129,193},{193,1... | collective-permute-start | bytes 98312 | tf_op jit(solution)/shard_map/ppermute | solution.py:505
  71.5 24.6 %copy-start.4 = (bf16[3584,256]{1,0:T(8,128)(2,1)S(1)}, bf16[3584,256]{1,0:T(8,128)(2,1)}, u32[]{:S(2)}) copy-start(bf16[3584,256]{1,0:T(8,128)(2,1)} %down_ref.3) | copy-start | bytes 5505028
  79.4 12.8 %all-to-all-start.3 = ((bf16[8,16,1024]{2,1,0:T(8,128)(2,1)}), bf16[8,16,1024]{2,1,0:T(8,128)(2,1)S(1)}, u32[]{:S(2)}, u32[]{:S(2)}) async-start(bf16[8,16,1024]{2,1,0:T(8,128)(2,1)} %shard_map.130), calls=%async_computation.3 | async-start | bytes 524288 | tf_op jit(solution)/shard_map/all_to_all | solution.py:409
  92.2 12.5 %collective-permute-start.11 = (bf16[144,896]{1,0:T(8,128)(2,1)S(1)}, bf16[144,896]{1,0:T(8,128)(2,1)S(1)}, u32[]{:S(2)}, u32[]{:S(2)}) collective-permute-start(bf16[144,896]{1,0:T(8,128)(2,1)S(1)} %shard_map.131.after_ref.own_ref), channel_id=1, source_target_pairs={{0,1},{1,2},{2,3},{3,0},{4,5},{5,6},{6,7},{7,4},{8,9},{9,10},{10,1... | collective-permute-start | bytes 774152 | tf_op jit(solution)/shard_map/ppermute | solution.py:584
  92.8 12.0 %collective-permute-start.12 = (bf16[144,896]{1,0:T(8,128)(2,1)S(1)}, bf16[144,896]{1,0:T(8,128)(2,1)S(1)}, u32[]{:S(2)}, u32[]{:S(2)}) collective-permute-start(bf16[144,896]{1,0:T(8,128)(2,1)S(1)} %shard_map.131.after_ref.own_ref), channel_id=1, source_target_pairs={{0,2},{1,3},{2,0},{3,1},{4,6},{5,7},{6,4},{7,5},{8,10},{9,11},{10,... | collective-permute-start | bytes 774152 | tf_op jit(solution)/shard_map/ppermute | solution.py:584
  96.0 8.8 %collective-permute-start.13 = (bf16[144,896]{1,0:T(8,128)(2,1)S(1)}, bf16[144,896]{1,0:T(8,128)(2,1)S(1)}, u32[]{:S(2)}, u32[]{:S(2)}) collective-permute-start(bf16[144,896]{1,0:T(8,128)(2,1)S(1)} %shard_map.131.after_ref.own_ref), channel_id=1, source_target_pairs={{0,3},{1,0},{2,1},{3,2},{4,7},{5,4},{6,5},{7,6},{8,11},{9,8},{10,9... | collective-permute-start | bytes 774152 | tf_op jit(solution)/shard_map/ppermute | solution.py:584
  (2 other events, 1.6 us)
where the time goes:
time: 122 us; the launch traced here: 121 us
  starting transfers between devices  44.9 us (37%)
  waiting for transfers between devices  26.6 us (22%)
  Pallas kernels  24.6 us (20%)
  blocking collectives  13.7 us (11%)
  local copies, waits for them, and re-layouts  5.01 us (4%)
  other arithmetic  5 us (4%)
    all_to_all x4, starting transfers between devices, exchange(): return lax.all_to_all(value, axes, 0, 0, tiled=True)  26.3 us
    all_to_all x4, waiting for transfers between devices, exchange(): return lax.all_to_all(value, axes, 0, 0, tiled=True)  16.4 us
    all_to_all x1, blocking collectives, exchange(): return lax.all_to_all(value, axes, 0, 0, tiled=True)  13.7 us
    pallas_call x1, Pallas kernels, on_device(): pl.pallas_call(delta_kernel, grid=(peers_y,), in_specs=[smem, hbm, full(c...  8.67 us
    ppermute x6, starting transfers between devices, turn(): lax.ppermute(value, axis, [(i, (i + k) % peers) for i in range(peers)])  6.19 us
    ppermute x6, waiting for transfers between devices, turn(): lax.ppermute(value, axis, [(i, (i + k) % peers) for i in range(peers)])  5.48 us
    pallas_call x1, Pallas kernels, on_device(): pl.pallas_call(first_kernel, in_specs=[smem, VMEM, hbm, hbm, hbm], out_sp...  5.27 us
    ppermute x4, starting transfers between devices, swap(): return lax.ppermute(value, 'y', [(y, y ^ mask) for y in range(peers_y)])  4.45 us
  transfers between devices with their start and end apart: 18, of which 11 were waited for; matrix products, arithmetic and copies ran while one was open for 6% of the time, Pallas kernels for 10%

commit v1 on v0

--- a/solution.py
+++ b/solution.py
@@ -114,69 +114,80 @@
     refs[-1][...] = total.astype(BF16)
 
 
-def project_kernel(x_ref, table_ref, after_ref, out_ref):
+def quarter_copies(order_ref, refs, scratch, sems, first):
+    wide = scratch[0].shape[2]
+    copies = []
+    for i in range(scratch[0].shape[0]):
+        units = pl.ds(pl.multiple_of(order_ref[first + i] * wide, SPAN), wide)
+        places = (refs[0].at[:, units], refs[1].at[:, units], refs[2].at[units, :])
+        copies.append(
+            [
+                pltpu.make_async_copy(place, to.at[i], sems.at[i, k])
+                for k, (place, to) in enumerate(zip(places, scratch, strict=True))
+            ]
+        )
+    for three in copies:
+        for copy in three:
+            copy.start()
+    return copies
+
+
+def quarter_parts(x_ref, scratch, i, copies):
+    feats = x_ref.shape[1] // 2
+    for copy in copies[i]:
+        copy.wait()
+    gates, ups, downs = scratch
+    tokens, cotangent = x_ref[:, :feats], x_ref[:, feats:]
+    return matmul(tokens, gates[i]), matmul(tokens, ups[i]), against(cotangent, downs[i])
+
+
+def first_kernel(
+    order_ref, x_ref, gate_ref, up_ref, down_ref, send_a, send_b, keep_a, keep_b, *scratch
+):
+    *scratch, sems = scratch
+    copies = quarter_copies(order_ref, (gate_ref, up_ref, down_ref), scratch, sems, 0)
+    half, wide = x_ref.shape[0] // 2, scratch[0].shape[2]
+    places = (
+        (send_a.at[0], keep_b),
+        (send_a.at[1], send_b.at[0]),
+        (keep_a, send_b.at[1]),
+    )
+    for i, (low, high) in enumerate(places):
+        for at, part in enumerate(quarter_parts(x_ref, scratch, i, copies)):
+            lanes = slice(at * wide, (at + 1) * wide)
+            low[:, lanes] = part[:half].astype(BF16)
+            high[:, lanes] = part[half:].astype(BF16)
+
+
+def own_kernel(
+    order_ref, x_ref, table_ref, gate_ref, up_ref, down_ref, after_ref, proj_ref, own_ref, *scratch
+):
     del after_ref
-    feats = x_ref.shape[1] // 2
+    *scratch, sems = scratch
+    copies = quarter_copies(order_ref, (gate_ref, up_ref, down_ref), scratch, sems, 3)
+    feats, wide = scratch[0].shape[1:]
     for which in range(2):
         values = x_ref[:, which * feats : (which + 1) * feats]
         lanes = slice(2 * which * SPAN, 2 * (which + 1) * SPAN)
-        out_ref[:, lanes] = matmul(values, table_ref[which]).astype(BF16)
-
-
-def first_kernel(
-    order_ref, x_ref, gate_ref, up_ref, down_ref, *refs
-):
-    out_refs, (gates, ups, downs, sems) = refs[:4], refs[4:]
-    _, feats, wide = gates.shape
-    half = x_ref.shape[0] // 2
-    copies = []
-    for i in range(gates.shape[0]):
-        units = pl.ds(pl.multiple_of(order_ref[i] * wide, SPAN), wide)
-        copies.append(
-            (
-                pltpu.make_async_copy(gate_ref.at[:, units], gates.at[i], sems.at[i, 0]),
-                pltpu.make_async_copy(up_ref.at[:, units], ups.at[i], sems.at[i, 1]),
-                pltpu.make_async_copy(down_ref.at[units, :], downs.at[i], sems.at[i, 2]),
-            )
-        )
-        for copy in copies[-1]:
-            copy.start()
-    tokens = x_ref[:, :feats]
-    cotangent = x_ref[:, feats:]
-    send_a, send_b, keep_a, keep_b = out_refs
-    places = (
-        ((send_a, 0), (keep_b, 0)),
-        ((send_a, 1), (send_b, 0)),
-        ((keep_a, 0), (send_b, 1)),
-        ((keep_a, 1), (keep_b, 1)),
-    )
-    for i, (low, high) in enumerate(places):
-        for copy in copies[i]:
-            copy.wait()
-        parts = (
-            matmul(tokens, gates[i]),
-            matmul(tokens, ups[i]),
-            against(cotangent, downs[i]),
-        )
-        for at, part in enumerate(parts):
-            lanes = slice(at * wide, (at + 1) * wide)
-            low[0][low[1], :, lanes] = part[:half].astype(BF16)
-            high[0][high[1], :, lanes] = part[half:].astype(BF16)
-
-
-def fold_kernel(keep_a, keep_b, got_a, got_b, send_a, send_b):
-    send_a[...] = (keep_a[0].astype(F32) + got_a[0].astype(F32)).astype(BF16)
-    send_b[...] = (keep_b[0].astype(F32) + got_b[0].astype(F32)).astype(BF16)
-
-
-def close_kernel(keep_a, keep_b, got_a, got_b, last_a, last_b, proj_ref, out_ref, proj_out):
+        proj_ref[:, lanes] = matmul(values, table_ref[which]).astype(BF16)
+    for at, part in enumerate(quarter_parts(x_ref, scratch, 0, copies)):
+        own_ref[:, at * wide : (at + 1) * wide] = part.astype(BF16)
+
+
+def fold_kernel(keep_a, keep_b, got_a, got_b, after_ref, send_a, send_b):
+    del after_ref
+    send_a[...] = (keep_a[...].astype(F32) + got_a[0].astype(F32)).astype(BF16)
+    send_b[...] = (keep_b[...].astype(F32) + got_b[0].astype(F32)).astype(BF16)
+
+
+def close_kernel(own_ref, got_a, got_b, last_a, last_b, proj_ref, out_ref, proj_out):
     proj_out[...] = proj_ref[...]
     half = last_a.shape[0]
     out_ref[:half] = (
-        keep_a[0].astype(F32) + got_a[0].astype(F32) + last_a[...].astype(F32)
+        own_ref[:half].astype(F32) + got_a[0].astype(F32) + last_a[...].astype(F32)
     ).astype(BF16)
     out_ref[half:] = (
-        keep_b[0].astype(F32) + got_b[0].astype(F32) + last_b[...].astype(F32)
+        own_ref[half:].astype(F32) + got_b[0].astype(F32) + last_b[...].astype(F32)
     ).astype(BF16)
 
 
@@ -324,7 +335,8 @@
         out_ref[c, :, wide:] = grads
 
 
-def regroup_kernel(in_ref, out_ref):
+def regroup_kernel(in_ref, after_ref, out_ref):
+    del after_ref
     peers, rows, _ = in_ref.shape
     wide = out_ref.shape[1]
     grads = jnp.zeros((rows, SPAN), F32)
@@ -337,7 +349,7 @@
     out_ref[peers * rows :, 2 * SPAN :] = jnp.zeros((rows, wide - 2 * SPAN), BF16)
 
 
-def last_kernel(own_ref, one_ref, two_ref, three_ref, weight_ref, out_ref):
+def last_kernel(own_ref, one_ref, two_ref, three_ref, near_ref, far_ref, out_ref):
     peers, rows, feats = out_ref.shape
     rows //= 2
     wide = own_ref.shape[1]
@@ -345,7 +357,8 @@
     total = jnp.zeros((count, feats), F32)
     grads = jnp.zeros((own_ref.shape[0] - count, SPAN), F32)
     for k, ref in enumerate((own_ref, one_ref, two_ref, three_ref)):
-        units = slice(k * wide, (k + 1) * wide)
+        weight_ref = (near_ref, far_ref)[k // 2]
+        units = slice(k % 2 * wide, (k % 2 + 1) * wide)
         total += matmul(ref[:count, :], weight_ref[units, :])
         grads += ref[count:, :SPAN].astype(F32) + ref[count:, SPAN : 2 * SPAN].astype(F32)
     high, low = split(grads)
@@ -448,31 +461,39 @@
         out_shape=jax.ShapeDtypeStruct((2, feats, 2 * SPAN), BF16),
         compiler_params=params(8),
     )(base_own)
+    def scratch(quarters):
+        return [
+            pltpu.VMEM((quarters, feats, wide), BF16),
+            pltpu.VMEM((quarters, feats, wide), BF16),
+            pltpu.VMEM((quarters, wide, feats), BF16),
+            pltpu.SemaphoreType.DMA((quarters, 3)),
+        ]
+
+    piece = jax.ShapeDtypeStruct((half, block), BF16)
     send_a, send_b, keep_a, keep_b = pl.pallas_call(
         first_kernel,
         in_specs=[smem, VMEM, hbm, hbm, hbm],
         out_specs=[VMEM] * 4,
-        out_shape=[pieces] * 4,
-        scratch_shapes=[
-            pltpu.VMEM((peers_y, feats, wide), BF16),
-            pltpu.VMEM((peers_y, feats, wide), BF16),
-            pltpu.VMEM((peers_y, wide, feats), BF16),
-            pltpu.SemaphoreType.DMA((peers_y, 3)),
-        ],
-        compiler_params=params(60),
+        out_shape=[pieces] * 2 + [piece] * 2,
+        scratch_shapes=scratch(peers_y - 1),
+        compiler_params=params(57),
     )(order, both, gate_weight, up_weight, down_weight)
 
     def swap(value, mask):
         return lax.ppermute(value, "y", [(y, y ^ mask) for y in range(peers_y)])
 
     got_a, got_b = swap(send_a, 1), swap(send_b, 3)
-    proj = pl.pallas_call(
-        project_kernel,
-        in_specs=[VMEM] * 2 + [anywhere],
-        out_specs=VMEM,
-        out_shape=jax.ShapeDtypeStruct((count, peers_y * SPAN), BF16),
-        compiler_params=params(8),
-    )(both, table, keep_a)
+    proj, mine = pl.pallas_call(
+        own_kernel,
+        in_specs=[smem, VMEM, VMEM, hbm, hbm, hbm, anywhere],
+        out_specs=[VMEM] * 2,
+        out_shape=[
+            jax.ShapeDtypeStruct((count, peers_y * SPAN), BF16),
+            jax.ShapeDtypeStruct((count, block), BF16),
+        ],
+        scratch_shapes=scratch(1),
+        compiler_params=params(57),
+    )(order, both, table, gate_weight, up_weight, down_weight, keep_a)
     proj = exchange(proj.reshape(peers_z, share, peers_y * SPAN), "z")
 
     freq, coefs = pl.pallas_call(
@@ -512,16 +533,16 @@
     send_a, send_b = pl.pallas_call(
         fold_kernel,
         grid=(1,),
-        in_specs=[whole(0), whole(0), whole(1), whole(0)],
+        in_specs=[full((half, block))] * 2 + [whole(1), whole(0), anywhere],
         out_specs=[full((half, block))] * 2,
         out_shape=[jax.ShapeDtypeStruct((half, block), BF16)] * 2,
         compiler_params=params(12),
-    )(keep_a, keep_b, got_a, got_b)
+    )(keep_a, keep_b, got_a, got_b, freq)
     last_a, last_b = swap(send_a, 3), swap(send_b, 1)
     sums, proj = pl.pallas_call(
         close_kernel,
         grid=(1,),
-        in_specs=[whole(1), whole(1), whole(0), whole(1)] + [full((half, block))] * 2
+        in_specs=[full((count, block)), whole(0), whole(1)] + [full((half, block))] * 2
         + [full(proj.shape)],
         out_specs=[full((count, block)), full(proj.shape)],
         out_shape=[
@@ -529,7 +550,7 @@
             jax.ShapeDtypeStruct(proj.shape, BF16),
         ],
         compiler_params=params(12),
-    )(keep_a, keep_b, got_a, got_b, last_a, last_b, proj)
+    )(mine, got_a, got_b, last_a, last_b, proj)
     proj = jnp.stack([proj, lax.ppermute(proj, "core", [(0, 1), (1, 0)])])
     proj = jnp.stack([proj] + [turn(proj, "x", 4, k) for k in (1, 2, 3)])
     chip = (lax.axis_index("x") - jnp.arange(4, dtype=jnp.int32)) & 3
@@ -545,52 +566,64 @@
         scratch_shapes=[pltpu.VMEM((2, SPAN, 2 * PAD), BF16)],
         compiler_params=params(12),
     )(source, sums, proj, coefs, jnp.stack([base_up, base_down]))
+    def updated(first, after):
+        return pl.pallas_call(
+            delta_kernel,
+            grid=(2,),
+            in_specs=[
+                smem,
+                hbm,
+                full(coefs.shape),
+                full(base_down.shape),
+                full(base_out.shape),
+                pl.BlockSpec((1,) + turns.shape[1:], lambda i: (i, 0, 0)),
+                anywhere,
+            ],
+            out_specs=pl.BlockSpec((wide, feats), lambda i: (i, 0)),
+            out_shape=jax.ShapeDtypeStruct((2 * wide, feats), BF16),
+            scratch_shapes=[
+                pltpu.VMEM((wide, 2 * PAD), BF16),
+                pltpu.VMEM((2, feats, PAD), F32),
+                pltpu.VMEM((feats, 2 * PAD), BF16),
+                pltpu.VMEM((2, wide, feats), BF16),
+                pltpu.SemaphoreType.DMA((2,)),
+            ],
+            compiler_params=params(20),
+            cost_estimate=pl.CostEstimate(
+                flops=4 << 30, bytes_accessed=8 << 20, transcendentals=0
+            ),
+        )(
+            sources[first : first + 2],
+            down_weight,
+            coefs,
+            base_down,
+            base_out,
+            turns[first : first + 2],
+            after,
+        )
+
+    near = updated(0, hidden)
     hidden = exchange(hidden, "z")
     hidden = pl.pallas_call(
         regroup_kernel,
-        in_specs=[VMEM],
+        in_specs=[VMEM, anywhere],
         out_specs=VMEM,
         out_shape=jax.ShapeDtypeStruct((count + share, wide), BF16),
         compiler_params=params(8),
-    )(hidden)
-    weight = pl.pallas_call(
-        delta_kernel,
-        grid=(peers_y,),
-        in_specs=[
-            smem,
-            hbm,
-            full(coefs.shape),
-            full(base_down.shape),
-            full(base_out.shape),
-            pl.BlockSpec((1,) + turns.shape[1:], lambda i: (i, 0, 0)),
-            anywhere,
-        ],
-        out_specs=pl.BlockSpec((wide, feats), lambda i: (i, 0)),
-        out_shape=jax.ShapeDtypeStruct((units, feats), BF16),
-        scratch_shapes=[
-            pltpu.VMEM((wide, 2 * PAD), BF16),
-            pltpu.VMEM((2, feats, PAD), F32),
-            pltpu.VMEM((feats, 2 * PAD), BF16),
-            pltpu.VMEM((peers_y, wide, feats), BF16),
-            pltpu.SemaphoreType.DMA((peers_y,)),
-        ],
-        compiler_params=params(20),
-        cost_estimate=pl.CostEstimate(
-            flops=6 << 30, bytes_accessed=8 << 20, transcendentals=0
-        ),
-    )(sources, down_weight, coefs, base_down, base_out, turns, hidden)
-
+    )(hidden, near)
+    far = updated(2, hidden)
     def shifted(k):
         return lax.ppermute(hidden, "y", [(y, (y + k) % peers_y) for y in range(peers_y)])
 
-    others = [shifted(1), shifted(2), shifted(3)]
+    two = shifted(2)
+    others = [shifted(1), two, shifted(3)]
     mixed = pl.pallas_call(
         last_kernel,
-        in_specs=[VMEM] * 5,
+        in_specs=[VMEM] * 6,
         out_specs=VMEM,
         out_shape=jax.ShapeDtypeStruct((peers_row, 2 * own, feats), BF16),
         compiler_params=params(12),
-    )(hidden, *others, weight)
+    )(hidden, *others, near, far)
     mixed = exchange(mixed, PLANE)
 
     return pl.pallas_call(

time: 122 us -> 120 us (0.984)
  waiting for transfers between devices: 26.6 us -> 17.5 us
  Pallas kernels: 24.6 us -> 28.9 us
  other arithmetic: 5 us -> 8.3 us
  starting transfers between devices: 44.9 us -> 42.8 us
  local copies, waits for them, and re-layouts: 5.01 us -> 6.37 us
    pallas_call x6 -> x7, Pallas kernels: 12.1 us -> 16.9 us  [the longest x2 10.8 us: updated(): pl.pallas_call(delta_kernel, grid=(2,), in_specs=[smem, hbm, full(coefs.s...]
    all_to_all x4, waiting for transfers between devices: 16.4 us -> 12.3 us  [exchange(): return lax.all_to_all(value, axes, 0, 0, tiled=True)]
    ppermute x4, waiting for transfers between devices: 3.88 us -> 0.18 us  [swap(): return lax.ppermute(value, 'y', [(y, y ^ mask) for y in range(peers_y)])]
    another operation x2, other arithmetic: 0.07 us -> 2.42 us  [waves(): return jnp.stack([jnp.cos(angle), jnp.sin(angle)], axis=axis)]
    unnamed x16 -> x26, local copies, waits for them, and re-layouts: 2.68 us -> 3.97 us
    cos x4 -> x3, other arithmetic: 2.43 us -> 2.71 us  [waves(): return jnp.stack([jnp.cos(angle), jnp.sin(angle)], axis=axis)]
  transfers between devices with their start and end apart: 18 -> 18, of which waited for: 11 -> 11; matrix products, arithmetic and copies ran while one was open for 6% -> 9% of each run, Pallas kernels for 10% -> 14%
where the time goes in v1:
time: 120 us; the launch traced here: 119 us
  starting transfers between devices  42.8 us (36%)
  Pallas kernels  28.9 us (24%)
  waiting for transfers between devices  17.5 us (15%)
  blocking collectives  14.1 us (12%)
  other arithmetic  8.3 us (7%)
  local copies, waits for them, and re-layouts  6.37 us (5%)
    all_to_all x4, starting transfers between devices, exchange(): return lax.all_to_all(value, axes, 0, 0, tiled=True)  25.7 us
    all_to_all x1, blocking collectives, exchange(): return lax.all_to_all(value, axes, 0, 0, tiled=True)  14.1 us
    all_to_all x4, waiting for transfers between devices, exchange(): return lax.all_to_all(value, axes, 0, 0, tiled=True)  12.3 us
    pallas_call x2, Pallas kernels, updated(): pl.pallas_call(delta_kernel, grid=(2,), in_specs=[smem, hbm, full(coefs.s...  10.8 us
    ppermute x6, starting transfers between devices, turn(): lax.ppermute(value, axis, [(i, (i + k) % peers) for i in range(peers)])  5.12 us
    pallas_call x1, Pallas kernels, on_device(): pl.pallas_call(first_kernel, in_specs=[smem, VMEM, hbm, hbm, hbm], out_sp...  4.69 us
    ppermute x4, starting transfers between devices, swap(): return lax.ppermute(value, 'y', [(y, y ^ mask) for y in range(peers_y)])  4.46 us
    ppermute x6, waiting for transfers between devices, turn(): lax.ppermute(value, axis, [(i, (i + k) % peers) for i in range(peers)])  4.44 us
  transfers between devices with their start and end apart: 18, of which 11 were waited for; matrix products, arithmetic and copies ran while one was open for 9% of the time, Pallas kernels for 14%

profile of v1, /device:TPU:1, one launch (start us, length us, event | category | flops | bytes accessed | tf_op | source)
XLA Modules:
  0.0 118.9 jit_solution(6376757040215645273)
XLA Ops:
  0.6 1.4 %shard_map.122 = bf16[8,16,512]{2,1,0:T(8,128)(2,1)} custom-call(bf16[16,256]{1,0:T(8,128)(2,1)} %tokens_ref.1, bf16[16,256]{1,0:T(8,128)(2,1)} %cotangent_ref.1), custom_call_target="tpu_custom_call" | custom-call | tf_op jit(solution)/shard_map/pallas_call | solution.py:437
  2.0 6.5 %all-to-all-start = ((bf16[8,16,512]{2,1,0:T(8,128)(2,1)}), bf16[8,16,512]{2,1,0:T(8,128)(2,1)S(1)}, u32[]{:S(2)}, u32[]{:S(2)}) async-start(bf16[8,16,512]{2,1,0:T(8,128)(2,1)} %shard_map.122), calls=%async_computation | async-start | bytes 262144 | tf_op jit(solution)/shard_map/all_to_all | solution.py:422
  11.5 2.3 %all-to-all-done = bf16[8,16,512]{2,1,0:T(8,128)(2,1)S(1)} async-done(((bf16[8,16,512]{2,1,0:T(8,128)(2,1)}), bf16[8,16,512]{2,1,0:T(8,128)(2,1)S(1)}, u32[]{:S(2)}, u32[]{:S(2)}) %all-to-all-start) | async-done | bytes 131104 | tf_op jit(solution)/shard_map/all_to_all | solution.py:422
  14.5 4.7 %shard_map.124 = (bf16[2,64,2688]{2,1,0:T(8,128)(2,1)}, bf16[2,64,2688]{2,1,0:T(8,128)(2,1)}, bf16[64,2688]{1,0:T(8,128)(2,1)}, bf16[64,2688]{1,0:T(8,128)(2,1)}) custom-call(s32[4]{0:T(128)} %broadcast_xor_fusion.order_ref, bf16[128,512]{1,0:T(8,128)(2,1)} %bitcast.28, bf16[256,3584]{1,0:T(8,128)(2,1)} %gate_ref.3, bf16[256,3584]{1,0:T(8,128)(2,1)} %up_ref.3, ...), custom_call_target="tpu_custom_call" | custom-call | tf_op jit(solution)/shard_map/pallas_call | solution.py:473
  19.8 1.9 %collective-permute-start.1 = (bf16[2,64,2688]{2,1,0:T(8,128)(2,1)}, bf16[2,64,2688]{2,1,0:T(8,128)(2,1)S(1)}, u32[]{:S(2)}, u32[]{:S(2)}) collective-permute-start(bf16[2,64,2688]{2,1,0:T(8,128)(2,1)} %get-tuple-element.17), channel_id=1, source_target_pairs={{0,3},{1,2},{2,1},{3,0},{4,7},{5,6},{6,5},{7,4},{8,11},{9,10},{10,... | collective-permute-start | bytes 2064392 | tf_op jit(solution)/shard_map/ppermute | solution.py:483
  22.7 3.8 %shard_map.125 = (bf16[128,512]{1,0:T(8,128)(2,1)}, bf16[128,2688]{1,0:T(8,128)(2,1)}) custom-call(s32[4]{0:T(128)} %broadcast_xor_fusion.order_ref, bf16[128,512]{1,0:T(8,128)(2,1)} %bitcast.29, bf16[2,256,256]{2,1,0:T(8,128)(2,1)} %copy-done.2, bf16[256,3584]{1,0:T(8,128)(2,1)} %gate_ref.3, bf16[256,3584]{1,0:T(8,128)(2,1)} %up_ref.3, ...), custom_call_target="tpu_custom_call" | custom-call | tf_op jit(solution)/shard_map/pallas_call | solution.py:486
  27.8 8.2 %all-to-all-start.1 = ((bf16[8,16,512]{2,1,0:T(8,128)(2,1)}), bf16[8,16,512]{2,1,0:T(8,128)(2,1)S(1)}, u32[]{:S(2)}, u32[]{:S(2)}) async-start(bf16[8,16,512]{2,1,0:T(8,128)(2,1)} %bitcast.30), calls=%async_computation.1 | async-start | bytes 262144 | tf_op jit(solution)/shard_map/all_to_all | solution.py:422
  38.6 1.9 %collective-permute-start.2 = (bf16[64,2688]{1,0:T(8,128)(2,1)}, bf16[64,2688]{1,0:T(8,128)(2,1)S(1)}, u32[]{:S(2)}, u32[]{:S(2)}) collective-permute-start(bf16[64,2688]{1,0:T(8,128)(2,1)} %get-tuple-element.20), channel_id=1, source_target_pairs={{0,3},{1,2},{2,1},{3,0},{4,7},{5,6},{6,5},{7,4},{8,11},{9,10},{10,... | collective-permute-start | bytes 1032200 | tf_op jit(solution)/shard_map/ppermute | solution.py:483
  40.5 1.9 %fusion.14 = (f32[1,32,1024]{2,1,0:T(8,128)S(1)}, f32[1,32,1024]{2,1,0:T(8,128)}, f32[1,32,1024]{2,1,0:T(8,128)}, f32[1,32,1024]{2,1,0:T(8,128)}) fusion(s32[1024]{0:T(1024)S(1)} %bitcast.37, s32[32]{0:T(128)S(1)} %get-tuple-element.43, s32[1024]{0:T(1024)S(1)} %bitcast.31), kind=kLoop, calls=%fused_computation.28 | loop fusion | flops 589824 | bytes 532608 | tf_op jit(solution)/shard_map/cos | solution.py:37
  42.4 1.6 %all-to-all-done.1 = bf16[8,16,512]{2,1,0:T(8,128)(2,1)S(1)} async-done(((bf16[8,16,512]{2,1,0:T(8,128)(2,1)}), bf16[8,16,512]{2,1,0:T(8,128)(2,1)S(1)}, u32[]{:S(2)}, u32[]{:S(2)}) %all-to-all-start.1) | async-done | bytes 131104 | tf_op jit(solution)/shard_map/all_to_all | solution.py:422
  44.4 1.6 %collective-permute-start.5 = (bf16[16,512]{1,0:T(8,128)(2,1)S(1)}, bf16[16,512]{1,0:T(8,128)(2,1)S(1)}, u32[]{:S(2)}, u32[]{:S(2)}) collective-permute-start(bf16[16,512]{1,0:T(8,128)(2,1)S(1)} %reduce_sum.12.refs_0_), channel_id=1, source_target_pairs={{0,2},{1,3},{2,0},{3,1},{4,6},{5,7},{6,4},{7,5},{8,10},{9,11},{10,... | collective-permute-start | bytes 49160 | tf_op jit(solution)/shard_map/ppermute | solution.py:526
  46.9 1.7 %pad_maximum_fusion.1 = (f32[2,32,1024]{2,1,0:T(8,128)S(1)}, f32[1,2,32,1024]{3,2,1,0:T(8,128)}) fusion(f32[1,32,1024]{2,1,0:T(8,128)} %get-tuple-element.51, f32[1,32,1024]{2,1,0:T(8,128)} %get-tuple-element.52), kind=kLoop, calls=%fused_computation.2 | loop fusion | flops 65536 | bytes 786432 | tf_op jit(solution)/shard_map/stack | solution.py:37
  50.5 7.6 %all-to-all-start.2 = ((bf16[8,16,2688]{2,1,0:T(8,128)(2,1)}), bf16[8,16,2688]{2,1,0:T(8,128)(2,1)S(1)}, u32[]{:S(2)}, u32[]{:S(2)}) async-start(bf16[8,16,2688]{2,1,0:T(8,128)(2,1)} %bitcast.6), calls=%async_computation.2 | async-start | bytes 1376256 | tf_op jit(solution)/shard_map/all_to_all | solution.py:422
  59.3 3.9 %collective-permute-start.7 = (bf16[16,512]{1,0:T(8,128)(2,1)S(1)}, bf16[16,512]{1,0:T(8,128)(2,1)S(1)}, u32[]{:S(2)}, u32[]{:S(2)}) collective-permute-start(bf16[16,512]{1,0:T(8,128)(2,1)S(1)} %get-tuple-element.24), channel_id=1, source_target_pairs={{0,32},{32,0},{1,33},{33,1},{2,34},{34,2},{3,35},{35,3},{4,36},{36... | collective-permute-start | bytes 49160 | tf_op jit(solution)/shard_map/ppermute | solution.py:554
  67.5 2.4 %collective-permute-done.9 = bf16[2,16,512]{2,1,0:T(8,128)(2,1)S(1)} collective-permute-done((bf16[2,16,512]{2,1,0:T(8,128)(2,1)S(1)}, bf16[2,16,512]{2,1,0:T(8,128)(2,1)S(1)}, u32[]{:S(2)}, u32[]{:S(2)}) %collective-permute-start.9) | collective-permute-done | bytes 32800 | tf_op jit(solution)/shard_map/ppermute | solution.py:526
  71.1 5.6 %all-to-all-done.2.sums_ref = bf16[8,16,2688]{2,1,0:T(8,128)(2,1)S(1)} async-done(((bf16[8,16,2688]{2,1,0:T(8,128)(2,1)}), bf16[8,16,2688]{2,1,0:T(8,128)(2,1)S(1)}, u32[]{:S(2)}, u32[]{:S(2)}) %all-to-all-start.2) | async-done | bytes 688160 | tf_op jit(solution)/shard_map/all_to_all | solution.py:422
  76.6 2.8 %shard_map.130.after_ref = bf16[8,16,1024]{2,1,0:T(8,128)(2,1)} custom-call(s32[6]{0:T(128)S(1)} %pad_add_fusion.source_ref, bf16[8,16,2688]{2,1,0:T(8,128)(2,1)S(1)} %all-to-all-done.2.sums_ref, bf16[4,2,16,512]{3,2,1,0:T(8,128)(2,1)S(1)} %pad_maximum_fusion.3.proj_ref, f32[2,1024]{1,0:T(2,128)S(1)} %copy-done.8, ...), custom_call_target="tpu_custom_call" | custom-call | tf_op jit(solution)/shard_map/pallas_call | solution.py:561
  79.4 3.4 %all-to-all-start.3 = ((bf16[8,16,1024]{2,1,0:T(8,128)(2,1)}), bf16[8,16,1024]{2,1,0:T(8,128)(2,1)S(1)}, u32[]{:S(2)}, u32[]{:S(2)}) async-start(bf16[8,16,1024]{2,1,0:T(8,128)(2,1)} %shard_map.130.after_ref), calls=%async_computation.3 | async-start | bytes 524288 | tf_op jit(solution)/shard_map/all_to_all | solution.py:422
  83.8 5.4 %shard_map.131.after_ref.near_ref = bf16[1792,256]{1,0:T(8,128)(2,1)S(1)} custom-call(s32[2]{0:T(128)S(1)} %get-tuple-element.50.order_ref, bf16[3584,256]{1,0:T(8,128)(2,1)S(1)} %copy-done, f32[2,1024]{1,0:T(2,128)S(1)} %copy-done.8, f32[2,32,1024]{2,1,0:T(8,128)S(1)} %get-tuple-element.26.base_ref, f32[2,32,1024]{2,1,0:T(8,128)S(1)} %copy-done.5, ...), custom_call_target="tpu_custom_call" | custom-call | flops 4294967296 | bytes 8388608 | tf_op jit(solution)/shard_map/pallas_call | solution.py:570
  89.2 3.0 %all-to-all-done.3.in_ref = bf16[8,16,1024]{2,1,0:T(8,128)(2,1)S(1)} async-done(((bf16[8,16,1024]{2,1,0:T(8,128)(2,1)}), bf16[8,16,1024]{2,1,0:T(8,128)(2,1)S(1)}, u32[]{:S(2)}, u32[]{:S(2)}) %all-to-all-start.3) | async-done | bytes 262176 | tf_op jit(solution)/shard_map/all_to_all | solution.py:422
  92.7 3.0 %collective-permute-start.12 = (bf16[144,896]{1,0:T(8,128)(2,1)S(1)}, bf16[144,896]{1,0:T(8,128)(2,1)S(1)}, u32[]{:S(2)}, u32[]{:S(2)}) collective-permute-start(bf16[144,896]{1,0:T(8,128)(2,1)S(1)} %shard_map.132.after_ref.own_ref), channel_id=1, source_target_pairs={{0,2},{1,3},{2,0},{3,1},{4,6},{5,7},{6,4},{7,5},{8,10},{9,11},{10,... | collective-permute-start | bytes 774152 | tf_op jit(solution)/shard_map/ppermute | solution.py:616
  96.7 5.4 %shard_map.133.far_ref = bf16[1792,256]{1,0:T(8,128)(2,1)S(1)} custom-call(s32[2]{0:T(128)S(1)} %get-tuple-element.49.order_ref, bf16[3584,256]{1,0:T(8,128)(2,1)S(1)} %copy-done, f32[2,1024]{1,0:T(2,128)S(1)} %copy-done.8, f32[2,32,1024]{2,1,0:T(8,128)S(1)} %get-tuple-element.26.base_ref, f32[2,32,1024]{2,1,0:T(8,128)S(1)} %copy-done.6, ...), custom_call_target="tpu_custom_call" | custom-call | flops 4294967296 | bytes 8388608 | tf_op jit(solution)/shard_map/pallas_call | solution.py:570
  103.1 14.1 %all_to_all.25.in_ref = bf16[8,32,256]{2,1,0:T(8,128)(2,1)} all-to-all(bf16[8,32,256]{2,1,0:T(8,128)(2,1)S(1)} %shard_map.134), channel_id=1, replica_groups=mesh['x'=4,'core'=2,'z'=8,'y'=4] {'x','core'}, dimensions={0} | all-to-all | bytes 262144 | tf_op jit(solution)/shard_map/all_to_all | solution.py:422
  117.2 1.7 %shard_map.135 = (bf16[16,256]{1,0:T(8,128)(2,1)}, f32[2,1000]{1,0:T(2,128)}) custom-call(bf16[8,32,256]{2,1,0:T(8,128)(2,1)} %all_to_all.25.in_ref, f32[2,1000]{1,0:T(2,128)} %first_ref.1, f32[2,1000]{1,0:T(2,128)} %second_ref.1), custom_call_target="tpu_custom_call" | custom-call | tf_op jit(solution)/shard_map/pallas_call | solution.py:629
  (85 shorter events, 22.5 us)
Async XLA Ops:
  2.0 11.8 %all-to-all-start = ((bf16[8,16,512]{2,1,0:T(8,128)(2,1)}), bf16[8,16,512]{2,1,0:T(8,128)(2,1)S(1)}, u32[]{:S(2)}, u32[]{:S(2)}) async-start(bf16[8,16,512]{2,1,0:T(8,128)(2,1)} %shard_map.122), calls=%async_computation | async-start | bytes 262144 | tf_op jit(solution)/shard_map/all_to_all | solution.py:422
  19.2 17.7 %collective-permute-start = (bf16[2,64,2688]{2,1,0:T(8,128)(2,1)}, bf16[2,64,2688]{2,1,0:T(8,128)(2,1)S(1)}, u32[]{:S(2)}, u32[]{:S(2)}) collective-permute-start(bf16[2,64,2688]{2,1,0:T(8,128)(2,1)} %get-tuple-element.16), channel_id=1, source_target_pairs={{0,1},{1,0},{2,3},{3,2},{4,5},{5,4},{6,7},{7,6},{8,9},{9,8},{10,11... | collective-permute-start | bytes 2064392 | tf_op jit(solution)/shard_map/ppermute | solution.py:483
  19.8 17.2 %collective-permute-start.1 = (bf16[2,64,2688]{2,1,0:T(8,128)(2,1)}, bf16[2,64,2688]{2,1,0:T(8,128)(2,1)S(1)}, u32[]{:S(2)}, u32[]{:S(2)}) collective-permute-start(bf16[2,64,2688]{2,1,0:T(8,128)(2,1)} %get-tuple-element.17), channel_id=1, source_target_pairs={{0,3},{1,2},{2,1},{3,0},{4,7},{5,6},{6,5},{7,4},{8,11},{9,10},{10,... | collective-permute-start | bytes 2064392 | tf_op jit(solution)/shard_map/ppermute | solution.py:483
  22.7 14.3 %copy-start.1 = (bf16[64,2688]{1,0:T(8,128)(2,1)S(1)}, bf16[64,2688]{1,0:T(8,128)(2,1)}, u32[]{:S(2)}) copy-start(bf16[64,2688]{1,0:T(8,128)(2,1)} %get-tuple-element.14.after_ref.keep_a) | copy-start | bytes 1032196
  22.7 14.3 %copy-start.4 = (bf16[64,2688]{1,0:T(8,128)(2,1)S(1)}, bf16[64,2688]{1,0:T(8,128)(2,1)}, u32[]{:S(2)}) copy-start(bf16[64,2688]{1,0:T(8,128)(2,1)} %get-tuple-element.18.keep_b) | copy-start | bytes 1032196
  27.8 16.1 %all-to-all-start.1 = ((bf16[8,16,512]{2,1,0:T(8,128)(2,1)}), bf16[8,16,512]{2,1,0:T(8,128)(2,1)S(1)}, u32[]{:S(2)}, u32[]{:S(2)}) async-start(bf16[8,16,512]{2,1,0:T(8,128)(2,1)} %bitcast.30), calls=%async_computation.1 | async-start | bytes 262144 | tf_op jit(solution)/shard_map/all_to_all | solution.py:422
  36.0 13.3 %copy-start.3 = (bf16[128,2688]{1,0:T(8,128)(2,1)S(1)}, bf16[128,2688]{1,0:T(8,128)(2,1)}, u32[]{:S(2)}) copy-start(bf16[128,2688]{1,0:T(8,128)(2,1)} %get-tuple-element.15.own_ref) | copy-start | bytes 2064388
  38.6 10.8 %collective-permute-start.2 = (bf16[64,2688]{1,0:T(8,128)(2,1)}, bf16[64,2688]{1,0:T(8,128)(2,1)S(1)}, u32[]{:S(2)}, u32[]{:S(2)}) collective-permute-start(bf16[64,2688]{1,0:T(8,128)(2,1)} %get-tuple-element.20), channel_id=1, source_target_pairs={{0,3},{1,2},{2,1},{3,0},{4,7},{5,6},{6,5},{7,4},{8,11},{9,10},{10,... | collective-permute-start | bytes 1032200 | tf_op jit(solution)/shard_map/ppermute | solution.py:483
  40.5 8.9 %collective-permute-start.3 = (bf16[64,2688]{1,0:T(8,128)(2,1)S(1)}, bf16[64,2688]{1,0:T(8,128)(2,1)S(1)}, u32[]{:S(2)}, u32[]{:S(2)}) collective-permute-start(bf16[64,2688]{1,0:T(8,128)(2,1)S(1)} %get-tuple-element.21), channel_id=1, source_target_pairs={{0,1},{1,0},{2,3},{3,2},{4,5},{5,4},{6,7},{7,6},{8,9},{9,8},{10,11... | collective-permute-start | bytes 1032200 | tf_op jit(solution)/shard_map/ppermute | solution.py:483
  44.0 4.7 %collective-permute-start.4 = (bf16[16,512]{1,0:T(8,128)(2,1)S(1)}, bf16[16,512]{1,0:T(8,128)(2,1)S(1)}, u32[]{:S(2)}, u32[]{:S(2)}) collective-permute-start(bf16[16,512]{1,0:T(8,128)(2,1)S(1)} %reduce_sum.12.refs_0_), channel_id=1, source_target_pairs={{0,1},{1,2},{2,3},{3,0},{4,5},{5,6},{6,7},{7,4},{8,9},{9,10},{10,1... | collective-permute-start | bytes 49160 | tf_op jit(solution)/shard_map/ppermute | solution.py:526
  44.4 4.3 %collective-permute-start.5 = (bf16[16,512]{1,0:T(8,128)(2,1)S(1)}, bf16[16,512]{1,0:T(8,128)(2,1)S(1)}, u32[]{:S(2)}, u32[]{:S(2)}) collective-permute-start(bf16[16,512]{1,0:T(8,128)(2,1)S(1)} %reduce_sum.12.refs_0_), channel_id=1, source_target_pairs={{0,2},{1,3},{2,0},{3,1},{4,6},{5,7},{6,4},{7,5},{8,10},{9,11},{10,... | collective-permute-start | bytes 49160 | tf_op jit(solution)/shard_map/ppermute | solution.py:526
  46.0 3.3 %collective-permute-start.6 = (bf16[16,512]{1,0:T(8,128)(2,1)S(1)}, bf16[16,512]{1,0:T(8,128)(2,1)S(1)}, u32[]{:S(2)}, u32[]{:S(2)}) collective-permute-start(bf16[16,512]{1,0:T(8,128)(2,1)S(1)} %reduce_sum.12.refs_0_), channel_id=1, source_target_pairs={{0,3},{1,0},{2,1},{3,2},{4,7},{5,4},{6,5},{7,6},{8,11},{9,8},{10,9... | collective-permute-start | bytes 49160 | tf_op jit(solution)/shard_map/ppermute | solution.py:526
  49.4 9.3 %copy-start.12 = (s32[32]{0:T(128)S(1)}, s32[32]{0:T(128)}, u32[]{:S(2)}) copy-start(s32[32]{0:T(128)} %copy-done.11) | copy-start | bytes 388
  50.5 26.1 %copy-start.8 = (f32[2,1024]{1,0:T(2,128)S(1)}, f32[2,1024]{1,0:T(2,128)}, u32[]{:S(2)}) copy-start(f32[2,1024]{1,0:T(2,128)} %get-tuple-element.25.coef_ref) | copy-start | bytes 24580
  50.5 26.1 %all-to-all-start.2 = ((bf16[8,16,2688]{2,1,0:T(8,128)(2,1)}), bf16[8,16,2688]{2,1,0:T(8,128)(2,1)S(1)}, u32[]{:S(2)}, u32[]{:S(2)}) async-start(bf16[8,16,2688]{2,1,0:T(8,128)(2,1)} %bitcast.6), calls=%async_computation.2 | async-start | bytes 1376256 | tf_op jit(solution)/shard_map/all_to_all | solution.py:422
  59.3 5.1 %collective-permute-start.7 = (bf16[16,512]{1,0:T(8,128)(2,1)S(1)}, bf16[16,512]{1,0:T(8,128)(2,1)S(1)}, u32[]{:S(2)}, u32[]{:S(2)}) collective-permute-start(bf16[16,512]{1,0:T(8,128)(2,1)S(1)} %get-tuple-element.24), channel_id=1, source_target_pairs={{0,32},{32,0},{1,33},{33,1},{2,34},{34,2},{3,35},{35,3},{4,36},{36... | collective-permute-start | bytes 49160 | tf_op jit(solution)/shard_map/ppermute | solution.py:554
  63.2 19.6 %copy-start = (bf16[3584,256]{1,0:T(8,128)(2,1)S(1)}, bf16[3584,256]{1,0:T(8,128)(2,1)}, u32[]{:S(2)}) copy-start(bf16[3584,256]{1,0:T(8,128)(2,1)} %down_ref.7) | copy-start | bytes 5505028
  64.4 3.1 %collective-permute-start.10 = (bf16[2,16,512]{2,1,0:T(8,128)(2,1)S(1)}, bf16[2,16,512]{2,1,0:T(8,128)(2,1)S(1)}, u32[]{:S(2)}, u32[]{:S(2)}) collective-permute-start(bf16[2,16,512]{2,1,0:T(8,128)(2,1)S(1)} %get-tuple-element.31), channel_id=1, source_target_pairs={{0,192},{64,0},{128,64},{192,128},{1,193},{65,1},{129,65},{193,129... | collective-permute-start | bytes 98312 | tf_op jit(solution)/shard_map/ppermute | solution.py:526
  65.4 4.6 %collective-permute-start.9 = (bf16[2,16,512]{2,1,0:T(8,128)(2,1)S(1)}, bf16[2,16,512]{2,1,0:T(8,128)(2,1)S(1)}, u32[]{:S(2)}, u32[]{:S(2)}) collective-permute-start(bf16[2,16,512]{2,1,0:T(8,128)(2,1)S(1)} %get-tuple-element.31), channel_id=1, source_target_pairs={{0,128},{64,192},{128,0},{192,64},{1,129},{65,193},{129,1},{193,65... | collective-permute-start | bytes 98312 | tf_op jit(solution)/shard_map/ppermute | solution.py:526
  66.5 4.5 %collective-permute-start.8 = (bf16[2,16,512]{2,1,0:T(8,128)(2,1)S(1)}, bf16[2,16,512]{2,1,0:T(8,128)(2,1)S(1)}, u32[]{:S(2)}, u32[]{:S(2)}) collective-permute-start(bf16[2,16,512]{2,1,0:T(8,128)(2,1)S(1)} %get-tuple-element.31), channel_id=1, source_target_pairs={{0,64},{64,128},{128,192},{192,0},{1,65},{65,129},{129,193},{193,1... | collective-permute-start | bytes 98312 | tf_op jit(solution)/shard_map/ppermute | solution.py:526
  79.4 12.8 %all-to-all-start.3 = ((bf16[8,16,1024]{2,1,0:T(8,128)(2,1)}), bf16[8,16,1024]{2,1,0:T(8,128)(2,1)S(1)}, u32[]{:S(2)}, u32[]{:S(2)}) async-start(bf16[8,16,1024]{2,1,0:T(8,128)(2,1)} %shard_map.130.after_ref), calls=%async_computation.3 | async-start | bytes 524288 | tf_op jit(solution)/shard_map/all_to_all | solution.py:422
  92.2 10.0 %collective-permute-start.11 = (bf16[144,896]{1,0:T(8,128)(2,1)S(1)}, bf16[144,896]{1,0:T(8,128)(2,1)S(1)}, u32[]{:S(2)}, u32[]{:S(2)}) collective-permute-start(bf16[144,896]{1,0:T(8,128)(2,1)S(1)} %shard_map.132.after_ref.own_ref), channel_id=1, source_target_pairs={{0,1},{1,2},{2,3},{3,0},{4,5},{5,6},{6,7},{7,4},{8,9},{9,10},{10,1... | collective-permute-start | bytes 774152 | tf_op jit(solution)/shard_map/ppermute | solution.py:616
  92.7 10.0 %collective-permute-start.12 = (bf16[144,896]{1,0:T(8,128)(2,1)S(1)}, bf16[144,896]{1,0:T(8,128)(2,1)S(1)}, u32[]{:S(2)}, u32[]{:S(2)}) collective-permute-start(bf16[144,896]{1,0:T(8,128)(2,1)S(1)} %shard_map.132.after_ref.own_ref), channel_id=1, source_target_pairs={{0,2},{1,3},{2,0},{3,1},{4,6},{5,7},{6,4},{7,5},{8,10},{9,11},{10,... | collective-permute-start | bytes 774152 | tf_op jit(solution)/shard_map/ppermute | solution.py:616
  95.7 7.0 %collective-permute-start.13 = (bf16[144,896]{1,0:T(8,128)(2,1)S(1)}, bf16[144,896]{1,0:T(8,128)(2,1)S(1)}, u32[]{:S(2)}, u32[]{:S(2)}) collective-permute-start(bf16[144,896]{1,0:T(8,128)(2,1)S(1)} %shard_map.132.after_ref.own_ref), channel_id=1, source_target_pairs={{0,3},{1,0},{2,1},{3,2},{4,7},{5,4},{6,5},{7,6},{8,11},{9,8},{10,9... | collective-permute-start | bytes 774152 | tf_op jit(solution)/shard_map/ppermute | solution.py:616
  (7 other events, 20.6 us)

commit v2 on v1

--- a/solution.py
+++ b/solution.py
@@ -141,22 +141,29 @@
     return matmul(tokens, gates[i]), matmul(tokens, ups[i]), against(cotangent, downs[i])
 
 
-def first_kernel(
-    order_ref, x_ref, gate_ref, up_ref, down_ref, send_a, send_b, keep_a, keep_b, *scratch
-):
+def put_halves(low, high, parts):
+    half = low.shape[0]
+    for at, part in enumerate(parts):
+        lanes = slice(at * part.shape[1], (at + 1) * part.shape[1])
+        low[:, lanes] = part[:half].astype(BF16)
+        high[:, lanes] = part[half:].astype(BF16)
+
+
+def first_kernel(order_ref, x_ref, gate_ref, up_ref, down_ref, send_a, send_b, *scratch):
     *scratch, sems = scratch
     copies = quarter_copies(order_ref, (gate_ref, up_ref, down_ref), scratch, sems, 0)
-    half, wide = x_ref.shape[0] // 2, scratch[0].shape[2]
-    places = (
-        (send_a.at[0], keep_b),
-        (send_a.at[1], send_b.at[0]),
-        (keep_a, send_b.at[1]),
-    )
-    for i, (low, high) in enumerate(places):
-        for at, part in enumerate(quarter_parts(x_ref, scratch, i, copies)):
-            lanes = slice(at * wide, (at + 1) * wide)
-            low[:, lanes] = part[:half].astype(BF16)
-            high[:, lanes] = part[half:].astype(BF16)
+    put_halves(send_a, send_b, quarter_parts(x_ref, scratch, 0, copies))
+
+
+def second_kernel(
+    order_ref, x_ref, gate_ref, up_ref, down_ref, after_ref, one_ref, three_ref, *scratch
+):
+    del after_ref
+    *scratch, sems = scratch
+    copies = quarter_copies(order_ref, (gate_ref, up_ref, down_ref), scratch, sems, 1)
+    half = x_ref.shape[0] // 2
+    for i, ref in enumerate((one_ref, three_ref)):
+        put_halves(ref.at[:half], ref.at[half:], quarter_parts(x_ref, scratch, i, copies))
 
 
 def own_kernel(
@@ -174,20 +181,19 @@
         own_ref[:, at * wide : (at + 1) * wide] = part.astype(BF16)
 
 
-def fold_kernel(keep_a, keep_b, got_a, got_b, after_ref, send_a, send_b):
-    del after_ref
-    send_a[...] = (keep_a[...].astype(F32) + got_a[0].astype(F32)).astype(BF16)
-    send_b[...] = (keep_b[...].astype(F32) + got_b[0].astype(F32)).astype(BF16)
-
-
-def close_kernel(own_ref, got_a, got_b, last_a, last_b, proj_ref, out_ref, proj_out):
+def fold_kernel(one_ref, three_ref, got_a, got_b, proj_ref, send_one, send_three, proj_out):
     proj_out[...] = proj_ref[...]
-    half = last_a.shape[0]
-    out_ref[:half] = (
-        own_ref[:half].astype(F32) + got_a[0].astype(F32) + last_a[...].astype(F32)
-    ).astype(BF16)
-    out_ref[half:] = (
-        own_ref[half:].astype(F32) + got_b[0].astype(F32) + last_b[...].astype(F32)
+    half = got_a.shape[0]
+    send_one[:half] = one_ref[:half]
+    send_one[half:] = (one_ref[half:].astype(F32) + got_b[...].astype(F32)).astype(BF16)
+    send_three[:half] = (three_ref[:half].astype(F32) + got_a[...].astype(F32)).astype(BF16)
+    send_three[half:] = three_ref[half:]
+
+
+def close_kernel(own_ref, got_one, got_three, proj_ref, out_ref, proj_out):
+    proj_out[...] = proj_ref[...]
+    out_ref[...] = (
+        own_ref[...].astype(F32) + got_one[...].astype(F32) + got_three[...].astype(F32)
     ).astype(BF16)
 
 
@@ -448,8 +454,7 @@
     smem = pl.BlockSpec(memory_space=pltpu.SMEM)
     hbm = pl.BlockSpec(memory_space=pltpu.HBM)
     anywhere = pl.BlockSpec(memory_space=pl.ANY)
-    order = y_index ^ jnp.array([1, 2, 3, 0], jnp.int32)
-    pieces = jax.ShapeDtypeStruct((2, half, block), BF16)
+    order = y_index ^ jnp.array([2, 1, 3, 0], jnp.int32)
 
     def full(shape):
         return pl.BlockSpec(shape, lambda i: (0,) * len(shape))
@@ -470,41 +475,47 @@
         ]
 
     piece = jax.ShapeDtypeStruct((half, block), BF16)
-    send_a, send_b, keep_a, keep_b = pl.pallas_call(
+    def swap(value, mask):
+        return lax.ppermute(value, "y", [(y, y ^ mask) for y in range(peers_y)])
+
+    early_a, early_b = pl.pallas_call(
         first_kernel,
         in_specs=[smem, VMEM, hbm, hbm, hbm],
-        out_specs=[VMEM] * 4,
-        out_shape=[pieces] * 2 + [piece] * 2,
-        scratch_shapes=scratch(peers_y - 1),
-        compiler_params=params(57),
+        out_specs=[VMEM] * 2,
+        out_shape=[piece] * 2,
+        scratch_shapes=scratch(1),
+        compiler_params=params(52),
     )(order, both, gate_weight, up_weight, down_weight)
-
-    def swap(value, mask):
-        return lax.ppermute(value, "y", [(y, y ^ mask) for y in range(peers_y)])
-
-    got_a, got_b = swap(send_a, 1), swap(send_b, 3)
+    got_early_a, got_early_b = swap(early_a, 1), swap(early_b, 3)
+    one, three = pl.pallas_call(
+        second_kernel,
+        in_specs=[smem, VMEM, hbm, hbm, hbm, VMEM],
+        out_specs=[VMEM] * 2,
+        out_shape=[jax.ShapeDtypeStruct((count, block), BF16)] * 2,
+        scratch_shapes=scratch(2),
+        compiler_params=params(52),
+    )(order, both, gate_weight, up_weight, down_weight, early_a)
     proj, mine = pl.pallas_call(
         own_kernel,
-        in_specs=[smem, VMEM, VMEM, hbm, hbm, hbm, anywhere],
+        in_specs=[smem, VMEM, VMEM, hbm, hbm, hbm, VMEM],
         out_specs=[VMEM] * 2,
         out_shape=[
             jax.ShapeDtypeStruct((count, peers_y * SPAN), BF16),
             jax.ShapeDtypeStruct((count, block), BF16),
         ],
         scratch_shapes=scratch(1),
-        compiler_params=params(57),
-    )(order, both, table, gate_weight, up_weight, down_weight, keep_a)
-    proj = exchange(proj.reshape(peers_z, share, peers_y * SPAN), "z")
+        compiler_params=params(52),
+    )(order, both, table, gate_weight, up_weight, down_weight, one)
 
     freq, coefs = pl.pallas_call(
         late_kernel,
-        in_specs=[VMEM] * 3 + [anywhere],
+        in_specs=[VMEM] * 4,
         out_specs=[VMEM] * 2,
         out_shape=[
             jax.ShapeDtypeStruct((4, PAD), jnp.int32),
             jax.ShapeDtypeStruct((2, PAD), F32),
         ],
-    )(spectral_rows, spectral_cols, coefficients, keep_a)
+    )(spectral_rows, spectral_cols, coefficients, one)
     tile_first = unit_first + y_index * wide
     base_up = phases(freq[2], tile_first, wide // SPAN, FF)
     base_down = phases(freq[1], tile_first, wide // SPAN, FF)
@@ -525,32 +536,28 @@
     def turn(value, axis, peers, k):
         return lax.ppermute(value, axis, [(i, (i + k) % peers) for i in range(peers)])
 
+    one, three, proj = pl.pallas_call(
+        fold_kernel,
+        in_specs=[VMEM] * 5,
+        out_specs=[VMEM] * 3,
+        out_shape=[jax.ShapeDtypeStruct((count, block), BF16)] * 2
+        + [jax.ShapeDtypeStruct(proj.shape, BF16)],
+        compiler_params=params(8),
+    )(one, three, got_early_a, got_early_b, proj)
+    got_one, got_three = swap(one, 1), swap(three, 3)
+    proj = exchange(proj.reshape(peers_z, share, peers_y * SPAN), "z")
     proj = jnp.sum(proj.astype(F32), axis=0).astype(BF16)
-    proj = added([proj] + [turn(proj, "y", peers_y, k) for k in (1, 2, 3)])
-    def whole(rows):
-        return pl.BlockSpec((1, half, block), lambda i: (rows, 0, 0))
-
-    send_a, send_b = pl.pallas_call(
-        fold_kernel,
-        grid=(1,),
-        in_specs=[full((half, block))] * 2 + [whole(1), whole(0), anywhere],
-        out_specs=[full((half, block))] * 2,
-        out_shape=[jax.ShapeDtypeStruct((half, block), BF16)] * 2,
-        compiler_params=params(12),
-    )(keep_a, keep_b, got_a, got_b, freq)
-    last_a, last_b = swap(send_a, 3), swap(send_b, 1)
     sums, proj = pl.pallas_call(
         close_kernel,
-        grid=(1,),
-        in_specs=[full((count, block)), whole(0), whole(1)] + [full((half, block))] * 2
-        + [full(proj.shape)],
-        out_specs=[full((count, block)), full(proj.shape)],
+        in_specs=[VMEM] * 4,
+        out_specs=[VMEM] * 2,
         out_shape=[
             jax.ShapeDtypeStruct((count, block), BF16),
             jax.ShapeDtypeStruct(proj.shape, BF16),
         ],
-        compiler_params=params(12),
-    )(mine, got_a, got_b, last_a, last_b, proj)
+        compiler_params=params(8),
+    )(mine, got_one, got_three, proj)
+    proj = added([proj] + [turn(proj, "y", peers_y, k) for k in (1, 2, 3)])
     proj = jnp.stack([proj, lax.ppermute(proj, "core", [(0, 1), (1, 0)])])
     proj = jnp.stack([proj] + [turn(proj, "x", 4, k) for k in (1, 2, 3)])
     chip = (lax.axis_index("x") - jnp.arange(4, dtype=jnp.int32)) & 3

time: 120 us -> 119 us (level)
  waiting for transfers between devices: 17.5 us -> 23.5 us
  other arithmetic: 8.3 us -> 5.03 us
  local copies, waits for them, and re-layouts: 6.37 us -> 4.32 us
  blocking collectives: 14.1 us -> 12.1 us
  starting transfers between devices: 42.8 us -> 44.2 us
    pallas_call x1, Pallas kernels: 4.69 us -> 2.34 us  [on_device(): pl.pallas_call(first_kernel, in_specs=[smem, VMEM, hbm, hbm, hbm], out_sp...]
    ppermute x4, waiting for transfers between devices: 0.18 us -> 2.36 us  [swap(): return lax.ppermute(value, 'y', [(y, y ^ mask) for y in range(peers_y)])]
    unnamed x26 -> x14, local copies, waits for them, and re-layouts: 3.97 us -> 1.92 us
    pallas_call x4 -> x5, Pallas kernels: 7.04 us -> 9.08 us  [the longest x1 2.83 us: on_device(): pl.pallas_call(second_kernel, in_specs=[smem, VMEM, hbm, hbm, hbm, VMEM],...]
    ppermute x3, waiting for transfers between devices: 0.53 us -> 2.57 us  [shifted(): lax.ppermute(hidden, 'y', [(y, (y + k) % peers_y) for y in range(peers_y)])]
    all_to_all x1, blocking collectives: 14.1 us -> 12.1 us  [exchange(): return lax.all_to_all(value, axes, 0, 0, tiled=True)]
    another operation x2, other arithmetic: 2.42 us -> 0.75 us  [waves(): return jnp.stack([jnp.cos(angle), jnp.sin(angle)], axis=axis)]
    ppermute x6, waiting for transfers between devices: 4.44 us -> 5.72 us  [turn(): lax.ppermute(value, axis, [(i, (i + k) % peers) for i in range(peers)])]
  transfers between devices with their start and end apart: 18 -> 18, of which waited for: 11 -> 14; matrix products, arithmetic and copies ran while one was open for 9% -> 6% of each run, Pallas kernels for 14% -> 15%
where the time goes in v2:
time: 119 us; the launch traced here: 118 us
  starting transfers between devices  44.2 us (37%)
  Pallas kernels  28.5 us (24%)
  waiting for transfers between devices  23.5 us (20%)
  blocking collectives  12.1 us (10%)
  other arithmetic  5.03 us (4%)
  local copies, waits for them, and re-layouts  4.32 us (4%)
    all_to_all x4, starting transfers between devices, exchange(): return lax.all_to_all(value, axes, 0, 0, tiled=True)  25.2 us
    all_to_all x1, blocking collectives, exchange(): return lax.all_to_all(value, axes, 0, 0, tiled=True)  12.1 us
    all_to_all x4, waiting for transfers between devices, exchange(): return lax.all_to_all(value, axes, 0, 0, tiled=True)  12 us
    pallas_call x2, Pallas kernels, updated(): pl.pallas_call(delta_kernel, grid=(2,), in_specs=[smem, hbm, full(coefs.s...  10.7 us
    ppermute x6, waiting for transfers between devices, turn(): lax.ppermute(value, axis, [(i, (i + k) % peers) for i in range(peers)])  5.72 us
    ppermute x6, starting transfers between devices, turn(): lax.ppermute(value, axis, [(i, (i + k) % peers) for i in range(peers)])  5.68 us
    ppermute x1, starting transfers between devices, on_device(): proj = jnp.stack([proj, lax.ppermute(proj, 'core', [(0, 1), (1, 0)])])  5.14 us
    ppermute x4, starting transfers between devices, swap(): return lax.ppermute(value, 'y', [(y, y ^ mask) for y in range(peers_y)])  4.46 us
  transfers between devices with their start and end apart: 18, of which 14 were waited for; matrix products, arithmetic and copies ran while one was open for 6% of the time, Pallas kernels for 15%

profile of v2, /device:TPU:1, one launch (start us, length us, event | category | flops | bytes accessed | tf_op | source)
XLA Modules:
  0.0 118.4 jit_solution(3626037777414919050)
XLA Ops:
  2.0 6.5 %all-to-all-start = ((bf16[8,16,512]{2,1,0:T(8,128)(2,1)}), bf16[8,16,512]{2,1,0:T(8,128)(2,1)S(1)}, u32[]{:S(2)}, u32[]{:S(2)}) async-start(bf16[8,16,512]{2,1,0:T(8,128)(2,1)} %shard_map.122), calls=%async_computation | async-start | bytes 262144 | tf_op jit(solution)/shard_map/all_to_all | solution.py:428
  11.0 2.8 %all-to-all-done = bf16[8,16,512]{2,1,0:T(8,128)(2,1)S(1)} async-done(((bf16[8,16,512]{2,1,0:T(8,128)(2,1)}), bf16[8,16,512]{2,1,0:T(8,128)(2,1)S(1)}, u32[]{:S(2)}, u32[]{:S(2)}) %all-to-all-start) | async-done | bytes 131104 | tf_op jit(solution)/shard_map/all_to_all | solution.py:428
  13.8 2.3 %shard_map.124 = (bf16[64,2688]{1,0:T(8,128)(2,1)S(1)}, bf16[64,2688]{1,0:T(8,128)(2,1)S(1)}) custom-call(s32[4]{0:T(128)S(1)} %broadcast_xor_fusion.order_ref, bf16[128,512]{1,0:T(8,128)(2,1)S(1)} %bitcast.27, bf16[256,3584]{1,0:T(8,128)(2,1)} %gate_ref.5, bf16[256,3584]{1,0:T(8,128)(2,1)} %up_ref.5, bf16[3584,256]{1,0:T(8,128)(2,1)} %down_ref.9), custom_call_target="tpu_custom_call" | custom-call | tf_op jit(solution)/shard_map/pallas_call | solution.py:481
  16.8 1.9 %collective-permute-start.1 = (bf16[64,2688]{1,0:T(8,128)(2,1)S(1)}, bf16[64,2688]{1,0:T(8,128)(2,1)S(1)}, u32[]{:S(2)}, u32[]{:S(2)}) collective-permute-start(bf16[64,2688]{1,0:T(8,128)(2,1)S(1)} %get-tuple-element.19), channel_id=1, source_target_pairs={{0,3},{1,2},{2,1},{3,0},{4,7},{5,6},{6,5},{7,4},{8,11},{9,10},{10,... | collective-permute-start | bytes 1032200 | tf_op jit(solution)/shard_map/ppermute | solution.py:479
  18.9 2.8 %shard_map.125 = (bf16[128,2688]{1,0:T(8,128)(2,1)S(1)}, bf16[128,2688]{1,0:T(8,128)(2,1)S(1)}) custom-call(s32[4]{0:T(128)S(1)} %broadcast_xor_fusion.order_ref, bf16[128,512]{1,0:T(8,128)(2,1)S(1)} %bitcast.28, bf16[256,3584]{1,0:T(8,128)(2,1)} %gate_ref.5, bf16[256,3584]{1,0:T(8,128)(2,1)} %up_ref.5, bf16[3584,256]{1,0:T(8,128)(2,1)} %down_ref.9, ...), custom_call_target="tpu_custom_call" | custom-call | tf_op jit(solution)/shard_map/pallas_call | solution.py:490
  21.7 2.4 %shard_map.126 = (bf16[128,512]{1,0:T(8,128)(2,1)S(1)}, bf16[128,2688]{1,0:T(8,128)(2,1)S(1)}) custom-call(s32[4]{0:T(128)S(1)} %broadcast_xor_fusion.order_ref, bf16[128,512]{1,0:T(8,128)(2,1)S(1)} %bitcast.29, bf16[2,256,256]{2,1,0:T(8,128)(2,1)S(1)} %shard_map.123.table_ref, bf16[256,3584]{1,0:T(8,128)(2,1)} %gate_ref.5, bf16[256,3584]{1,0:T(8,128)(2,1)} %up_ref.5, ...), custom_call_target="tpu_custom_call" | custom-call | tf_op jit(solution)/shard_map/pallas_call | solution.py:498
  27.5 1.9 %collective-permute-start.3 = (bf16[128,2688]{1,0:T(8,128)(2,1)S(1)}, bf16[128,2688]{1,0:T(8,128)(2,1)S(1)}, u32[]{:S(2)}, u32[]{:S(2)}) collective-permute-start(bf16[128,2688]{1,0:T(8,128)(2,1)S(1)} %get-tuple-element.22), channel_id=1, source_target_pairs={{0,3},{1,2},{2,1},{3,0},{4,7},{5,6},{6,5},{7,4},{8,11},{9,10},{10,... | collective-permute-start | bytes 2064392 | tf_op jit(solution)/shard_map/ppermute | solution.py:479
  29.5 1.8 %shard_map.130 = (s32[4,1024]{1,0:T(4,128)}, f32[2,1024]{1,0:T(2,128)}) custom-call(s32[2,1000]{1,0:T(2,128)} %rows_ref.1, s32[2,1000]{1,0:T(2,128)} %cols_ref.1, f32[2,1000]{1,0:T(2,128)} %coef_ref.1, bf16[128,2688]{1,0:T(8,128)(2,1)} %copy-done.1), custom_call_target="tpu_custom_call" | custom-call | tf_op jit(solution)/shard_map/pallas_call | solution.py:510
  32.1 8.2 %all-to-all-start.1 = ((bf16[8,16,512]{2,1,0:T(8,128)(2,1)}), bf16[8,16,512]{2,1,0:T(8,128)(2,1)S(1)}, u32[]{:S(2)}, u32[]{:S(2)}) async-start(bf16[8,16,512]{2,1,0:T(8,128)(2,1)} %bitcast.5), calls=%async_computation.1 | async-start | bytes 262144 | tf_op jit(solution)/shard_map/all_to_all | solution.py:428
  40.3 1.9 %fusion.14 = (f32[1,32,1024]{2,1,0:T(8,128)S(1)}, f32[1,32,1024]{2,1,0:T(8,128)}, f32[1,32,1024]{2,1,0:T(8,128)S(1)}, f32[1,32,1024]{2,1,0:T(8,128)}) fusion(s32[1024]{0:T(1024)S(1)} %bitcast.37, s32[32]{0:T(128)S(1)} %get-tuple-element.45, s32[1024]{0:T(1024)S(1)} %bitcast.31), kind=kLoop, calls=%fused_computation.28 | loop fusion | flops 589824 | bytes 532608 | tf_op jit(solution)/shard_map/cos | solution.py:37
  42.2 6.0 %all-to-all-done.1 = bf16[8,16,512]{2,1,0:T(8,128)(2,1)S(1)} async-done(((bf16[8,16,512]{2,1,0:T(8,128)(2,1)}), bf16[8,16,512]{2,1,0:T(8,128)(2,1)S(1)}, u32[]{:S(2)}, u32[]{:S(2)}) %all-to-all-start.1) | async-done | bytes 131104 | tf_op jit(solution)/shard_map/all_to_all | solution.py:428
  49.4 3.5 %all-to-all-start.2 = ((bf16[8,16,2688]{2,1,0:T(8,128)(2,1)}), bf16[8,16,2688]{2,1,0:T(8,128)(2,1)S(1)}, u32[]{:S(2)}, u32[]{:S(2)}) async-start(bf16[8,16,2688]{2,1,0:T(8,128)(2,1)} %bitcast.6), calls=%async_computation.2 | async-start | bytes 1376256 | tf_op jit(solution)/shard_map/all_to_all | solution.py:428
  55.1 2.0 %collective-permute-start.5 = (bf16[16,512]{1,0:T(8,128)(2,1)S(1)}, bf16[16,512]{1,0:T(8,128)(2,1)S(1)}, u32[]{:S(2)}, u32[]{:S(2)}) collective-permute-start(bf16[16,512]{1,0:T(8,128)(2,1)S(1)} %get-tuple-element.25.refs_0_), channel_id=1, source_target_pairs={{0,2},{1,3},{2,0},{3,1},{4,6},{5,7},{6,4},{7,5},{8,10},{9,11},{10,... | collective-permute-start | bytes 49160 | tf_op jit(solution)/shard_map/ppermute | solution.py:537
  59.8 5.1 %collective-permute-start.7 = (bf16[16,512]{1,0:T(8,128)(2,1)S(1)}, bf16[16,512]{1,0:T(8,128)(2,1)S(1)}, u32[]{:S(2)}, u32[]{:S(2)}) collective-permute-start(bf16[16,512]{1,0:T(8,128)(2,1)S(1)} %shard_map.129), channel_id=1, source_target_pairs={{0,32},{32,0},{1,33},{33,1},{2,34},{34,2},{3,35},{35,3},{4,36},{36... | collective-permute-start | bytes 49160 | tf_op jit(solution)/shard_map/ppermute | solution.py:561
  68.8 2.1 %collective-permute-done.9 = bf16[2,16,512]{2,1,0:T(8,128)(2,1)S(1)} collective-permute-done((bf16[2,16,512]{2,1,0:T(8,128)(2,1)S(1)}, bf16[2,16,512]{2,1,0:T(8,128)(2,1)S(1)}, u32[]{:S(2)}, u32[]{:S(2)}) %collective-permute-start.9) | collective-permute-done | bytes 32800 | tf_op jit(solution)/shard_map/ppermute | solution.py:537
  72.4 2.7 %shard_map.131.after_ref = bf16[8,16,1024]{2,1,0:T(8,128)(2,1)} custom-call(s32[6]{0:T(128)S(1)} %pad_add_fusion.source_ref, bf16[8,16,2688]{2,1,0:T(8,128)(2,1)S(1)} %all-to-all-done.2.sums_ref, bf16[4,2,16,512]{3,2,1,0:T(8,128)(2,1)S(1)} %pad_maximum_fusion.3.proj_ref, f32[2,1024]{1,0:T(2,128)S(1)} %copy-done.4, ...), custom_call_target="tpu_custom_call" | custom-call | tf_op jit(solution)/shard_map/pallas_call | solution.py:568
  75.1 6.9 %all-to-all-start.3 = ((bf16[8,16,1024]{2,1,0:T(8,128)(2,1)}), bf16[8,16,1024]{2,1,0:T(8,128)(2,1)S(1)}, u32[]{:S(2)}, u32[]{:S(2)}) async-start(bf16[8,16,1024]{2,1,0:T(8,128)(2,1)} %shard_map.131.after_ref), calls=%async_computation.3 | async-start | bytes 524288 | tf_op jit(solution)/shard_map/all_to_all | solution.py:428
  83.0 5.3 %shard_map.132.after_ref.near_ref = bf16[1792,256]{1,0:T(8,128)(2,1)S(1)} custom-call(s32[2]{0:T(128)S(1)} %get-tuple-element.52.order_ref, bf16[3584,256]{1,0:T(8,128)(2,1)S(1)} %copy-done, f32[2,1024]{1,0:T(2,128)S(1)} %copy-done.4, f32[2,32,1024]{2,1,0:T(8,128)S(1)} %get-tuple-element.28.base_ref, f32[2,32,1024]{2,1,0:T(8,128)S(1)} %copy-done.2, ...), custom_call_target="tpu_custom_call" | custom-call | flops 4294967296 | bytes 8388608 | tf_op jit(solution)/shard_map/pallas_call | solution.py:577
  88.4 3.2 %all-to-all-done.3.in_ref = bf16[8,16,1024]{2,1,0:T(8,128)(2,1)S(1)} async-done(((bf16[8,16,1024]{2,1,0:T(8,128)(2,1)}), bf16[8,16,1024]{2,1,0:T(8,128)(2,1)S(1)}, u32[]{:S(2)}, u32[]{:S(2)}) %all-to-all-start.3) | async-done | bytes 262176 | tf_op jit(solution)/shard_map/all_to_all | solution.py:428
  92.5 2.8 %collective-permute-start.12 = (bf16[144,896]{1,0:T(8,128)(2,1)S(1)}, bf16[144,896]{1,0:T(8,128)(2,1)S(1)}, u32[]{:S(2)}, u32[]{:S(2)}) collective-permute-start(bf16[144,896]{1,0:T(8,128)(2,1)S(1)} %shard_map.133.after_ref.own_ref), channel_id=1, source_target_pairs={{0,2},{1,3},{2,0},{3,1},{4,6},{5,7},{6,4},{7,5},{8,10},{9,11},{10,... | collective-permute-start | bytes 774152 | tf_op jit(solution)/shard_map/ppermute | solution.py:623
  96.3 5.3 %shard_map.134.far_ref = bf16[1792,256]{1,0:T(8,128)(2,1)S(1)} custom-call(s32[2]{0:T(128)S(1)} %get-tuple-element.51.order_ref, bf16[3584,256]{1,0:T(8,128)(2,1)S(1)} %copy-done, f32[2,1024]{1,0:T(2,128)S(1)} %copy-done.4, f32[2,32,1024]{2,1,0:T(8,128)S(1)} %get-tuple-element.28.base_ref, f32[2,32,1024]{2,1,0:T(8,128)S(1)} %copy-done.3, ...), custom_call_target="tpu_custom_call" | custom-call | flops 4294967296 | bytes 8388608 | tf_op jit(solution)/shard_map/pallas_call | solution.py:577
  101.6 1.8 %collective-permute-done.12.two_ref = bf16[144,896]{1,0:T(8,128)(2,1)S(1)} collective-permute-done((bf16[144,896]{1,0:T(8,128)(2,1)S(1)}, bf16[144,896]{1,0:T(8,128)(2,1)S(1)}, u32[]{:S(2)}, u32[]{:S(2)}) %collective-permute-start.12) | collective-permute-done | bytes 258080 | tf_op jit(solution)/shard_map/ppermute | solution.py:623
  104.7 12.1 %all_to_all.25.in_ref = bf16[8,32,256]{2,1,0:T(8,128)(2,1)} all-to-all(bf16[8,32,256]{2,1,0:T(8,128)(2,1)S(1)} %shard_map.135), channel_id=1, replica_groups=mesh['x'=4,'core'=2,'z'=8,'y'=4] {'x','core'}, dimensions={0} | all-to-all | bytes 262144 | tf_op jit(solution)/shard_map/all_to_all | solution.py:428
  116.7 1.7 %shard_map.136 = (bf16[16,256]{1,0:T(8,128)(2,1)}, f32[2,1000]{1,0:T(2,128)}) custom-call(bf16[8,32,256]{2,1,0:T(8,128)(2,1)} %all_to_all.25.in_ref, f32[2,1000]{1,0:T(2,128)} %first_ref.1, f32[2,1000]{1,0:T(2,128)} %second_ref.1), custom_call_target="tpu_custom_call" | custom-call | tf_op jit(solution)/shard_map/pallas_call | solution.py:636
  (74 shorter events, 24.4 us)
Async XLA Ops:
  2.0 11.8 %all-to-all-start = ((bf16[8,16,512]{2,1,0:T(8,128)(2,1)}), bf16[8,16,512]{2,1,0:T(8,128)(2,1)S(1)}, u32[]{:S(2)}, u32[]{:S(2)}) async-start(bf16[8,16,512]{2,1,0:T(8,128)(2,1)} %shard_map.122), calls=%async_computation | async-start | bytes 262144 | tf_op jit(solution)/shard_map/all_to_all | solution.py:428
  16.2 8.8 %collective-permute-start = (bf16[64,2688]{1,0:T(8,128)(2,1)S(1)}, bf16[64,2688]{1,0:T(8,128)(2,1)S(1)}, u32[]{:S(2)}, u32[]{:S(2)}) collective-permute-start(bf16[64,2688]{1,0:T(8,128)(2,1)S(1)} %get-tuple-element.15.after_ref), channel_id=1, source_target_pairs={{0,1},{1,0},{2,3},{3,2},{4,5},{5,4},{6,7},{7,6},{8,9},{9,8},{10,11... | collective-permute-start | bytes 1032200 | tf_op jit(solution)/shard_map/ppermute | solution.py:479
  16.8 9.6 %collective-permute-start.1 = (bf16[64,2688]{1,0:T(8,128)(2,1)S(1)}, bf16[64,2688]{1,0:T(8,128)(2,1)S(1)}, u32[]{:S(2)}, u32[]{:S(2)}) collective-permute-start(bf16[64,2688]{1,0:T(8,128)(2,1)S(1)} %get-tuple-element.19), channel_id=1, source_target_pairs={{0,3},{1,2},{2,1},{3,0},{4,7},{5,6},{6,5},{7,4},{8,11},{9,10},{10,... | collective-permute-start | bytes 1032200 | tf_op jit(solution)/shard_map/ppermute | solution.py:479
  21.7 4.7 %copy-start.1 = (bf16[128,2688]{1,0:T(8,128)(2,1)}, bf16[128,2688]{1,0:T(8,128)(2,1)S(1)}, u32[]{:S(2)}) copy-start(bf16[128,2688]{1,0:T(8,128)(2,1)S(1)} %get-tuple-element.16.after_ref.one_ref) | copy-start | bytes 2064388
  27.5 20.8 %collective-permute-start.2 = (bf16[128,2688]{1,0:T(8,128)(2,1)}, bf16[128,2688]{1,0:T(8,128)(2,1)S(1)}, u32[]{:S(2)}, u32[]{:S(2)}) collective-permute-start(bf16[128,2688]{1,0:T(8,128)(2,1)} %get-tuple-element.21), channel_id=1, source_target_pairs={{0,1},{1,0},{2,3},{3,2},{4,5},{5,4},{6,7},{7,6},{8,9},{9,8},{10,11... | collective-permute-start | bytes 2064392 | tf_op jit(solution)/shard_map/ppermute | solution.py:479
  27.5 20.8 %collective-permute-start.3 = (bf16[128,2688]{1,0:T(8,128)(2,1)S(1)}, bf16[128,2688]{1,0:T(8,128)(2,1)S(1)}, u32[]{:S(2)}, u32[]{:S(2)}) collective-permute-start(bf16[128,2688]{1,0:T(8,128)(2,1)S(1)} %get-tuple-element.22), channel_id=1, source_target_pairs={{0,3},{1,2},{2,1},{3,0},{4,7},{5,6},{6,5},{7,4},{8,11},{9,10},{10,... | collective-permute-start | bytes 2064392 | tf_op jit(solution)/shard_map/ppermute | solution.py:479
  32.1 16.1 %all-to-all-start.1 = ((bf16[8,16,512]{2,1,0:T(8,128)(2,1)}), bf16[8,16,512]{2,1,0:T(8,128)(2,1)S(1)}, u32[]{:S(2)}, u32[]{:S(2)}) async-start(bf16[8,16,512]{2,1,0:T(8,128)(2,1)} %bitcast.5), calls=%async_computation.1 | async-start | bytes 262144 | tf_op jit(solution)/shard_map/all_to_all | solution.py:428
  48.3 4.8 %copy-start.6 = (f32[1,32,1024]{2,1,0:T(8,128)S(1)}, f32[1,32,1024]{2,1,0:T(8,128)}, u32[]{:S(2)}) copy-start(f32[1,32,1024]{2,1,0:T(8,128)} %get-tuple-element.54) | copy-start | bytes 393220
  48.3 9.5 %copy-start.5 = (f32[1,32,1024]{2,1,0:T(8,128)S(1)}, f32[1,32,1024]{2,1,0:T(8,128)}, u32[]{:S(2)}) copy-start(f32[1,32,1024]{2,1,0:T(8,128)} %get-tuple-element.42) | copy-start | bytes 393220
  49.4 23.0 %all-to-all-start.2 = ((bf16[8,16,2688]{2,1,0:T(8,128)(2,1)}), bf16[8,16,2688]{2,1,0:T(8,128)(2,1)S(1)}, u32[]{:S(2)}, u32[]{:S(2)}) async-start(bf16[8,16,2688]{2,1,0:T(8,128)(2,1)} %bitcast.6), calls=%async_computation.2 | async-start | bytes 1376256 | tf_op jit(solution)/shard_map/all_to_all | solution.py:428
  53.1 19.3 %copy-start.4 = (f32[2,1024]{1,0:T(2,128)S(1)}, f32[2,1024]{1,0:T(2,128)}, u32[]{:S(2)}) copy-start(f32[2,1024]{1,0:T(2,128)} %get-tuple-element.26.coef_ref) | copy-start | bytes 24580
  54.2 3.9 %collective-permute-start.4 = (bf16[16,512]{1,0:T(8,128)(2,1)S(1)}, bf16[16,512]{1,0:T(8,128)(2,1)S(1)}, u32[]{:S(2)}, u32[]{:S(2)}) collective-permute-start(bf16[16,512]{1,0:T(8,128)(2,1)S(1)} %get-tuple-element.25.refs_0_), channel_id=1, source_target_pairs={{0,1},{1,2},{2,3},{3,0},{4,5},{5,6},{6,7},{7,4},{8,9},{9,10},{10,1... | collective-permute-start | bytes 49160 | tf_op jit(solution)/shard_map/ppermute | solution.py:537
  55.1 4.1 %collective-permute-start.5 = (bf16[16,512]{1,0:T(8,128)(2,1)S(1)}, bf16[16,512]{1,0:T(8,128)(2,1)S(1)}, u32[]{:S(2)}, u32[]{:S(2)}) collective-permute-start(bf16[16,512]{1,0:T(8,128)(2,1)S(1)} %get-tuple-element.25.refs_0_), channel_id=1, source_target_pairs={{0,2},{1,3},{2,0},{3,1},{4,6},{5,7},{6,4},{7,5},{8,10},{9,11},{10,... | collective-permute-start | bytes 49160 | tf_op jit(solution)/shard_map/ppermute | solution.py:537
  57.2 2.6 %collective-permute-start.6 = (bf16[16,512]{1,0:T(8,128)(2,1)S(1)}, bf16[16,512]{1,0:T(8,128)(2,1)S(1)}, u32[]{:S(2)}, u32[]{:S(2)}) collective-permute-start(bf16[16,512]{1,0:T(8,128)(2,1)S(1)} %get-tuple-element.25.refs_0_), channel_id=1, source_target_pairs={{0,3},{1,0},{2,1},{3,2},{4,7},{5,4},{6,5},{7,6},{8,11},{9,8},{10,9... | collective-permute-start | bytes 49160 | tf_op jit(solution)/shard_map/ppermute | solution.py:537
  59.8 6.0 %collective-permute-start.7 = (bf16[16,512]{1,0:T(8,128)(2,1)S(1)}, bf16[16,512]{1,0:T(8,128)(2,1)S(1)}, u32[]{:S(2)}, u32[]{:S(2)}) collective-permute-start(bf16[16,512]{1,0:T(8,128)(2,1)S(1)} %shard_map.129), channel_id=1, source_target_pairs={{0,32},{32,0},{1,33},{33,1},{2,34},{34,2},{3,35},{35,3},{4,36},{36... | collective-permute-start | bytes 49160 | tf_op jit(solution)/shard_map/ppermute | solution.py:561
  64.9 17.2 %copy-start = (bf16[3584,256]{1,0:T(8,128)(2,1)S(1)}, bf16[3584,256]{1,0:T(8,128)(2,1)}, u32[]{:S(2)}) copy-start(bf16[3584,256]{1,0:T(8,128)(2,1)} %down_ref.9) | copy-start | bytes 5505028
  65.7 3.1 %collective-permute-start.10 = (bf16[2,16,512]{2,1,0:T(8,128)(2,1)S(1)}, bf16[2,16,512]{2,1,0:T(8,128)(2,1)S(1)}, u32[]{:S(2)}, u32[]{:S(2)}) collective-permute-start(bf16[2,16,512]{2,1,0:T(8,128)(2,1)S(1)} %get-tuple-element.33), channel_id=1, source_target_pairs={{0,192},{64,0},{128,64},{192,128},{1,193},{65,1},{129,65},{193,129... | collective-permute-start | bytes 98312 | tf_op jit(solution)/shard_map/ppermute | solution.py:537
  66.6 4.3 %collective-permute-start.9 = (bf16[2,16,512]{2,1,0:T(8,128)(2,1)S(1)}, bf16[2,16,512]{2,1,0:T(8,128)(2,1)S(1)}, u32[]{:S(2)}, u32[]{:S(2)}) collective-permute-start(bf16[2,16,512]{2,1,0:T(8,128)(2,1)S(1)} %get-tuple-element.33), channel_id=1, source_target_pairs={{0,128},{64,192},{128,0},{192,64},{1,129},{65,193},{129,1},{193,65... | collective-permute-start | bytes 98312 | tf_op jit(solution)/shard_map/ppermute | solution.py:537
  67.8 4.5 %collective-permute-start.8 = (bf16[2,16,512]{2,1,0:T(8,128)(2,1)S(1)}, bf16[2,16,512]{2,1,0:T(8,128)(2,1)S(1)}, u32[]{:S(2)}, u32[]{:S(2)}) collective-permute-start(bf16[2,16,512]{2,1,0:T(8,128)(2,1)S(1)} %get-tuple-element.33), channel_id=1, source_target_pairs={{0,64},{64,128},{128,192},{192,0},{1,65},{65,129},{129,193},{193,1... | collective-permute-start | bytes 98312 | tf_op jit(solution)/shard_map/ppermute | solution.py:537
  75.1 16.5 %all-to-all-start.3 = ((bf16[8,16,1024]{2,1,0:T(8,128)(2,1)}), bf16[8,16,1024]{2,1,0:T(8,128)(2,1)S(1)}, u32[]{:S(2)}, u32[]{:S(2)}) async-start(bf16[8,16,1024]{2,1,0:T(8,128)(2,1)} %shard_map.131.after_ref), calls=%async_computation.3 | async-start | bytes 524288 | tf_op jit(solution)/shard_map/all_to_all | solution.py:428
  82.1 1.0 copy-start.2
  91.6 10.0 %collective-permute-start.11 = (bf16[144,896]{1,0:T(8,128)(2,1)S(1)}, bf16[144,896]{1,0:T(8,128)(2,1)S(1)}, u32[]{:S(2)}, u32[]{:S(2)}) collective-permute-start(bf16[144,896]{1,0:T(8,128)(2,1)S(1)} %shard_map.133.after_ref.own_ref), channel_id=1, source_target_pairs={{0,1},{1,2},{2,3},{3,0},{4,5},{5,6},{6,7},{7,4},{8,9},{9,10},{10,1... | collective-permute-start | bytes 774152 | tf_op jit(solution)/shard_map/ppermute | solution.py:623
  92.5 10.9 %collective-permute-start.12 = (bf16[144,896]{1,0:T(8,128)(2,1)S(1)}, bf16[144,896]{1,0:T(8,128)(2,1)S(1)}, u32[]{:S(2)}, u32[]{:S(2)}) collective-permute-start(bf16[144,896]{1,0:T(8,128)(2,1)S(1)} %shard_map.133.after_ref.own_ref), channel_id=1, source_target_pairs={{0,2},{1,3},{2,0},{3,1},{4,6},{5,7},{6,4},{7,5},{8,10},{9,11},{10,... | collective-permute-start | bytes 774152 | tf_op jit(solution)/shard_map/ppermute | solution.py:623
  95.2 9.0 %collective-permute-start.13 = (bf16[144,896]{1,0:T(8,128)(2,1)S(1)}, bf16[144,896]{1,0:T(8,128)(2,1)S(1)}, u32[]{:S(2)}, u32[]{:S(2)}) collective-permute-start(bf16[144,896]{1,0:T(8,128)(2,1)S(1)} %shard_map.133.after_ref.own_ref), channel_id=1, source_target_pairs={{0,3},{1,0},{2,1},{3,2},{4,7},{5,4},{6,5},{7,6},{8,11},{9,8},{10,9... | collective-permute-start | bytes 774152 | tf_op jit(solution)/shard_map/ppermute | solution.py:623
  (1 other events, 0.9 us)

commit v3 on v2

--- a/solution.py
+++ b/solution.py
@@ -613,7 +613,7 @@
     hidden = exchange(hidden, "z")
     hidden = pl.pallas_call(
         regroup_kernel,
-        in_specs=[VMEM, anywhere],
+        in_specs=[VMEM] * 2,
         out_specs=VMEM,
         out_shape=jax.ShapeDtypeStruct((count + share, wide), BF16),
         compiler_params=params(8),

time: 119 us -> 119 us (level)
  no operation moved by 1% of the time
where the time goes in v3:
time: 119 us; the launch traced here: 118 us
  starting transfers between devices  44.2 us (37%)
  Pallas kernels  28.5 us (24%)
  waiting for transfers between devices  23.5 us (20%)
  blocking collectives  12.1 us (10%)
  other arithmetic  5.03 us (4%)
  local copies, waits for them, and re-layouts  4.32 us (4%)
    all_to_all x4, starting transfers between devices, exchange(): return lax.all_to_all(value, axes, 0, 0, tiled=True)  25.2 us
    all_to_all x1, blocking collectives, exchange(): return lax.all_to_all(value, axes, 0, 0, tiled=True)  12.1 us
    all_to_all x4, waiting for transfers between devices, exchange(): return lax.all_to_all(value, axes, 0, 0, tiled=True)  12 us
    pallas_call x2, Pallas kernels, updated(): pl.pallas_call(delta_kernel, grid=(2,), in_specs=[smem, hbm, full(coefs.s...  10.7 us
    ppermute x6, waiting for transfers between devices, turn(): lax.ppermute(value, axis, [(i, (i + k) % peers) for i in range(peers)])  5.72 us
    ppermute x6, starting transfers between devices, turn(): lax.ppermute(value, axis, [(i, (i + k) % peers) for i in range(peers)])  5.68 us
    ppermute x1, starting transfers between devices, on_device(): proj = jnp.stack([proj, lax.ppermute(proj, 'core', [(0, 1), (1, 0)])])  5.14 us
    ppermute x4, starting transfers between devices, swap(): return lax.ppermute(value, 'y', [(y, y ^ mask) for y in range(peers_y)])  4.46 us
  transfers between devices with their start and end apart: 18, of which 14 were waited for; matrix products, arithmetic and copies ran while one was open for 6% of the time, Pallas kernels for 15%

profile of v3, /device:TPU:1, one launch (start us, length us, event | category | flops | bytes accessed | tf_op | source)
XLA Modules:
  0.0 118.4 jit_solution(3626037777414919050)
XLA Ops:
  2.0 6.5 %all-to-all-start = ((bf16[8,16,512]{2,1,0:T(8,128)(2,1)}), bf16[8,16,512]{2,1,0:T(8,128)(2,1)S(1)}, u32[]{:S(2)}, u32[]{:S(2)}) async-start(bf16[8,16,512]{2,1,0:T(8,128)(2,1)} %shard_map.122), calls=%async_computation | async-start | bytes 262144 | tf_op jit(solution)/shard_map/all_to_all | solution.py:428
  11.0 2.8 %all-to-all-done = bf16[8,16,512]{2,1,0:T(8,128)(2,1)S(1)} async-done(((bf16[8,16,512]{2,1,0:T(8,128)(2,1)}), bf16[8,16,512]{2,1,0:T(8,128)(2,1)S(1)}, u32[]{:S(2)}, u32[]{:S(2)}) %all-to-all-start) | async-done | bytes 131104 | tf_op jit(solution)/shard_map/all_to_all | solution.py:428
  13.8 2.3 %shard_map.124 = (bf16[64,2688]{1,0:T(8,128)(2,1)S(1)}, bf16[64,2688]{1,0:T(8,128)(2,1)S(1)}) custom-call(s32[4]{0:T(128)S(1)} %broadcast_xor_fusion.order_ref, bf16[128,512]{1,0:T(8,128)(2,1)S(1)} %bitcast.27, bf16[256,3584]{1,0:T(8,128)(2,1)} %gate_ref.5, bf16[256,3584]{1,0:T(8,128)(2,1)} %up_ref.5, bf16[3584,256]{1,0:T(8,128)(2,1)} %down_ref.9), custom_call_target="tpu_custom_call" | custom-call | tf_op jit(solution)/shard_map/pallas_call | solution.py:481
  16.8 1.9 %collective-permute-start.1 = (bf16[64,2688]{1,0:T(8,128)(2,1)S(1)}, bf16[64,2688]{1,0:T(8,128)(2,1)S(1)}, u32[]{:S(2)}, u32[]{:S(2)}) collective-permute-start(bf16[64,2688]{1,0:T(8,128)(2,1)S(1)} %get-tuple-element.19), channel_id=1, source_target_pairs={{0,3},{1,2},{2,1},{3,0},{4,7},{5,6},{6,5},{7,4},{8,11},{9,10},{10,... | collective-permute-start | bytes 1032200 | tf_op jit(solution)/shard_map/ppermute | solution.py:479
  18.9 2.8 %shard_map.125 = (bf16[128,2688]{1,0:T(8,128)(2,1)S(1)}, bf16[128,2688]{1,0:T(8,128)(2,1)S(1)}) custom-call(s32[4]{0:T(128)S(1)} %broadcast_xor_fusion.order_ref, bf16[128,512]{1,0:T(8,128)(2,1)S(1)} %bitcast.28, bf16[256,3584]{1,0:T(8,128)(2,1)} %gate_ref.5, bf16[256,3584]{1,0:T(8,128)(2,1)} %up_ref.5, bf16[3584,256]{1,0:T(8,128)(2,1)} %down_ref.9, ...), custom_call_target="tpu_custom_call" | custom-call | tf_op jit(solution)/shard_map/pallas_call | solution.py:490
  21.7 2.4 %shard_map.126 = (bf16[128,512]{1,0:T(8,128)(2,1)S(1)}, bf16[128,2688]{1,0:T(8,128)(2,1)S(1)}) custom-call(s32[4]{0:T(128)S(1)} %broadcast_xor_fusion.order_ref, bf16[128,512]{1,0:T(8,128)(2,1)S(1)} %bitcast.29, bf16[2,256,256]{2,1,0:T(8,128)(2,1)S(1)} %shard_map.123.table_ref, bf16[256,3584]{1,0:T(8,128)(2,1)} %gate_ref.5, bf16[256,3584]{1,0:T(8,128)(2,1)} %up_ref.5, ...), custom_call_target="tpu_custom_call" | custom-call | tf_op jit(solution)/shard_map/pallas_call | solution.py:498
  27.5 1.9 %collective-permute-start.3 = (bf16[128,2688]{1,0:T(8,128)(2,1)S(1)}, bf16[128,2688]{1,0:T(8,128)(2,1)S(1)}, u32[]{:S(2)}, u32[]{:S(2)}) collective-permute-start(bf16[128,2688]{1,0:T(8,128)(2,1)S(1)} %get-tuple-element.22), channel_id=1, source_target_pairs={{0,3},{1,2},{2,1},{3,0},{4,7},{5,6},{6,5},{7,4},{8,11},{9,10},{10,... | collective-permute-start | bytes 2064392 | tf_op jit(solution)/shard_map/ppermute | solution.py:479
  29.5 1.8 %shard_map.130 = (s32[4,1024]{1,0:T(4,128)}, f32[2,1024]{1,0:T(2,128)}) custom-call(s32[2,1000]{1,0:T(2,128)} %rows_ref.1, s32[2,1000]{1,0:T(2,128)} %cols_ref.1, f32[2,1000]{1,0:T(2,128)} %coef_ref.1, bf16[128,2688]{1,0:T(8,128)(2,1)} %copy-done.1), custom_call_target="tpu_custom_call" | custom-call | tf_op jit(solution)/shard_map/pallas_call | solution.py:510
  32.1 8.2 %all-to-all-start.1 = ((bf16[8,16,512]{2,1,0:T(8,128)(2,1)}), bf16[8,16,512]{2,1,0:T(8,128)(2,1)S(1)}, u32[]{:S(2)}, u32[]{:S(2)}) async-start(bf16[8,16,512]{2,1,0:T(8,128)(2,1)} %bitcast.5), calls=%async_computation.1 | async-start | bytes 262144 | tf_op jit(solution)/shard_map/all_to_all | solution.py:428
  40.3 1.9 %fusion.14 = (f32[1,32,1024]{2,1,0:T(8,128)S(1)}, f32[1,32,1024]{2,1,0:T(8,128)}, f32[1,32,1024]{2,1,0:T(8,128)S(1)}, f32[1,32,1024]{2,1,0:T(8,128)}) fusion(s32[1024]{0:T(1024)S(1)} %bitcast.37, s32[32]{0:T(128)S(1)} %get-tuple-element.45, s32[1024]{0:T(1024)S(1)} %bitcast.31), kind=kLoop, calls=%fused_computation.28 | loop fusion | flops 589824 | bytes 532608 | tf_op jit(solution)/shard_map/cos | solution.py:37
  42.2 6.0 %all-to-all-done.1 = bf16[8,16,512]{2,1,0:T(8,128)(2,1)S(1)} async-done(((bf16[8,16,512]{2,1,0:T(8,128)(2,1)}), bf16[8,16,512]{2,1,0:T(8,128)(2,1)S(1)}, u32[]{:S(2)}, u32[]{:S(2)}) %all-to-all-start.1) | async-done | bytes 131104 | tf_op jit(solution)/shard_map/all_to_all | solution.py:428
  49.4 3.5 %all-to-all-start.2 = ((bf16[8,16,2688]{2,1,0:T(8,128)(2,1)}), bf16[8,16,2688]{2,1,0:T(8,128)(2,1)S(1)}, u32[]{:S(2)}, u32[]{:S(2)}) async-start(bf16[8,16,2688]{2,1,0:T(8,128)(2,1)} %bitcast.6), calls=%async_computation.2 | async-start | bytes 1376256 | tf_op jit(solution)/shard_map/all_to_all | solution.py:428
  55.1 2.0 %collective-permute-start.5 = (bf16[16,512]{1,0:T(8,128)(2,1)S(1)}, bf16[16,512]{1,0:T(8,128)(2,1)S(1)}, u32[]{:S(2)}, u32[]{:S(2)}) collective-permute-start(bf16[16,512]{1,0:T(8,128)(2,1)S(1)} %get-tuple-element.25.refs_0_), channel_id=1, source_target_pairs={{0,2},{1,3},{2,0},{3,1},{4,6},{5,7},{6,4},{7,5},{8,10},{9,11},{10,... | collective-permute-start | bytes 49160 | tf_op jit(solution)/shard_map/ppermute | solution.py:537
  59.8 5.1 %collective-permute-start.7 = (bf16[16,512]{1,0:T(8,128)(2,1)S(1)}, bf16[16,512]{1,0:T(8,128)(2,1)S(1)}, u32[]{:S(2)}, u32[]{:S(2)}) collective-permute-start(bf16[16,512]{1,0:T(8,128)(2,1)S(1)} %shard_map.129), channel_id=1, source_target_pairs={{0,32},{32,0},{1,33},{33,1},{2,34},{34,2},{3,35},{35,3},{4,36},{36... | collective-permute-start | bytes 49160 | tf_op jit(solution)/shard_map/ppermute | solution.py:561
  68.8 2.1 %collective-permute-done.9 = bf16[2,16,512]{2,1,0:T(8,128)(2,1)S(1)} collective-permute-done((bf16[2,16,512]{2,1,0:T(8,128)(2,1)S(1)}, bf16[2,16,512]{2,1,0:T(8,128)(2,1)S(1)}, u32[]{:S(2)}, u32[]{:S(2)}) %collective-permute-start.9) | collective-permute-done | bytes 32800 | tf_op jit(solution)/shard_map/ppermute | solution.py:537
  72.4 2.7 %shard_map.131.after_ref = bf16[8,16,1024]{2,1,0:T(8,128)(2,1)} custom-call(s32[6]{0:T(128)S(1)} %pad_add_fusion.source_ref, bf16[8,16,2688]{2,1,0:T(8,128)(2,1)S(1)} %all-to-all-done.2.sums_ref, bf16[4,2,16,512]{3,2,1,0:T(8,128)(2,1)S(1)} %pad_maximum_fusion.3.proj_ref, f32[2,1024]{1,0:T(2,128)S(1)} %copy-done.4, ...), custom_call_target="tpu_custom_call" | custom-call | tf_op jit(solution)/shard_map/pallas_call | solution.py:568
  75.1 6.9 %all-to-all-start.3 = ((bf16[8,16,1024]{2,1,0:T(8,128)(2,1)}), bf16[8,16,1024]{2,1,0:T(8,128)(2,1)S(1)}, u32[]{:S(2)}, u32[]{:S(2)}) async-start(bf16[8,16,1024]{2,1,0:T(8,128)(2,1)} %shard_map.131.after_ref), calls=%async_computation.3 | async-start | bytes 524288 | tf_op jit(solution)/shard_map/all_to_all | solution.py:428
  83.0 5.3 %shard_map.132.after_ref.near_ref = bf16[1792,256]{1,0:T(8,128)(2,1)S(1)} custom-call(s32[2]{0:T(128)S(1)} %get-tuple-element.52.order_ref, bf16[3584,256]{1,0:T(8,128)(2,1)S(1)} %copy-done, f32[2,1024]{1,0:T(2,128)S(1)} %copy-done.4, f32[2,32,1024]{2,1,0:T(8,128)S(1)} %get-tuple-element.28.base_ref, f32[2,32,1024]{2,1,0:T(8,128)S(1)} %copy-done.2, ...), custom_call_target="tpu_custom_call" | custom-call | flops 4294967296 | bytes 8388608 | tf_op jit(solution)/shard_map/pallas_call | solution.py:577
  88.4 3.2 %all-to-all-done.3.in_ref = bf16[8,16,1024]{2,1,0:T(8,128)(2,1)S(1)} async-done(((bf16[8,16,1024]{2,1,0:T(8,128)(2,1)}), bf16[8,16,1024]{2,1,0:T(8,128)(2,1)S(1)}, u32[]{:S(2)}, u32[]{:S(2)}) %all-to-all-start.3) | async-done | bytes 262176 | tf_op jit(solution)/shard_map/all_to_all | solution.py:428
  92.5 2.8 %collective-permute-start.12 = (bf16[144,896]{1,0:T(8,128)(2,1)S(1)}, bf16[144,896]{1,0:T(8,128)(2,1)S(1)}, u32[]{:S(2)}, u32[]{:S(2)}) collective-permute-start(bf16[144,896]{1,0:T(8,128)(2,1)S(1)} %shard_map.133.after_ref.own_ref), channel_id=1, source_target_pairs={{0,2},{1,3},{2,0},{3,1},{4,6},{5,7},{6,4},{7,5},{8,10},{9,11},{10,... | collective-permute-start | bytes 774152 | tf_op jit(solution)/shard_map/ppermute | solution.py:623
  96.3 5.3 %shard_map.134.far_ref = bf16[1792,256]{1,0:T(8,128)(2,1)S(1)} custom-call(s32[2]{0:T(128)S(1)} %get-tuple-element.51.order_ref, bf16[3584,256]{1,0:T(8,128)(2,1)S(1)} %copy-done, f32[2,1024]{1,0:T(2,128)S(1)} %copy-done.4, f32[2,32,1024]{2,1,0:T(8,128)S(1)} %get-tuple-element.28.base_ref, f32[2,32,1024]{2,1,0:T(8,128)S(1)} %copy-done.3, ...), custom_call_target="tpu_custom_call" | custom-call | flops 4294967296 | bytes 8388608 | tf_op jit(solution)/shard_map/pallas_call | solution.py:577
  101.6 1.8 %collective-permute-done.12.two_ref = bf16[144,896]{1,0:T(8,128)(2,1)S(1)} collective-permute-done((bf16[144,896]{1,0:T(8,128)(2,1)S(1)}, bf16[144,896]{1,0:T(8,128)(2,1)S(1)}, u32[]{:S(2)}, u32[]{:S(2)}) %collective-permute-start.12) | collective-permute-done | bytes 258080 | tf_op jit(solution)/shard_map/ppermute | solution.py:623
  104.7 12.1 %all_to_all.25.in_ref = bf16[8,32,256]{2,1,0:T(8,128)(2,1)} all-to-all(bf16[8,32,256]{2,1,0:T(8,128)(2,1)S(1)} %shard_map.135), channel_id=1, replica_groups=mesh['x'=4,'core'=2,'z'=8,'y'=4] {'x','core'}, dimensions={0} | all-to-all | bytes 262144 | tf_op jit(solution)/shard_map/all_to_all | solution.py:428
  116.7 1.7 %shard_map.136 = (bf16[16,256]{1,0:T(8,128)(2,1)}, f32[2,1000]{1,0:T(2,128)}) custom-call(bf16[8,32,256]{2,1,0:T(8,128)(2,1)} %all_to_all.25.in_ref, f32[2,1000]{1,0:T(2,128)} %first_ref.1, f32[2,1000]{1,0:T(2,128)} %second_ref.1), custom_call_target="tpu_custom_call" | custom-call | tf_op jit(solution)/shard_map/pallas_call | solution.py:636
  (74 shorter events, 24.4 us)
Async XLA Ops:
  2.0 11.8 %all-to-all-start = ((bf16[8,16,512]{2,1,0:T(8,128)(2,1)}), bf16[8,16,512]{2,1,0:T(8,128)(2,1)S(1)}, u32[]{:S(2)}, u32[]{:S(2)}) async-start(bf16[8,16,512]{2,1,0:T(8,128)(2,1)} %shard_map.122), calls=%async_computation | async-start | bytes 262144 | tf_op jit(solution)/shard_map/all_to_all | solution.py:428
  16.2 8.8 %collective-permute-start = (bf16[64,2688]{1,0:T(8,128)(2,1)S(1)}, bf16[64,2688]{1,0:T(8,128)(2,1)S(1)}, u32[]{:S(2)}, u32[]{:S(2)}) collective-permute-start(bf16[64,2688]{1,0:T(8,128)(2,1)S(1)} %get-tuple-element.15.after_ref), channel_id=1, source_target_pairs={{0,1},{1,0},{2,3},{3,2},{4,5},{5,4},{6,7},{7,6},{8,9},{9,8},{10,11... | collective-permute-start | bytes 1032200 | tf_op jit(solution)/shard_map/ppermute | solution.py:479
  16.8 9.6 %collective-permute-start.1 = (bf16[64,2688]{1,0:T(8,128)(2,1)S(1)}, bf16[64,2688]{1,0:T(8,128)(2,1)S(1)}, u32[]{:S(2)}, u32[]{:S(2)}) collective-permute-start(bf16[64,2688]{1,0:T(8,128)(2,1)S(1)} %get-tuple-element.19), channel_id=1, source_target_pairs={{0,3},{1,2},{2,1},{3,0},{4,7},{5,6},{6,5},{7,4},{8,11},{9,10},{10,... | collective-permute-start | bytes 1032200 | tf_op jit(solution)/shard_map/ppermute | solution.py:479
  21.7 4.7 %copy-start.1 = (bf16[128,2688]{1,0:T(8,128)(2,1)}, bf16[128,2688]{1,0:T(8,128)(2,1)S(1)}, u32[]{:S(2)}) copy-start(bf16[128,2688]{1,0:T(8,128)(2,1)S(1)} %get-tuple-element.16.after_ref.one_ref) | copy-start | bytes 2064388
  27.5 20.8 %collective-permute-start.2 = (bf16[128,2688]{1,0:T(8,128)(2,1)}, bf16[128,2688]{1,0:T(8,128)(2,1)S(1)}, u32[]{:S(2)}, u32[]{:S(2)}) collective-permute-start(bf16[128,2688]{1,0:T(8,128)(2,1)} %get-tuple-element.21), channel_id=1, source_target_pairs={{0,1},{1,0},{2,3},{3,2},{4,5},{5,4},{6,7},{7,6},{8,9},{9,8},{10,11... | collective-permute-start | bytes 2064392 | tf_op jit(solution)/shard_map/ppermute | solution.py:479
  27.5 20.8 %collective-permute-start.3 = (bf16[128,2688]{1,0:T(8,128)(2,1)S(1)}, bf16[128,2688]{1,0:T(8,128)(2,1)S(1)}, u32[]{:S(2)}, u32[]{:S(2)}) collective-permute-start(bf16[128,2688]{1,0:T(8,128)(2,1)S(1)} %get-tuple-element.22), channel_id=1, source_target_pairs={{0,3},{1,2},{2,1},{3,0},{4,7},{5,6},{6,5},{7,4},{8,11},{9,10},{10,... | collective-permute-start | bytes 2064392 | tf_op jit(solution)/shard_map/ppermute | solution.py:479
  32.1 16.1 %all-to-all-start.1 = ((bf16[8,16,512]{2,1,0:T(8,128)(2,1)}), bf16[8,16,512]{2,1,0:T(8,128)(2,1)S(1)}, u32[]{:S(2)}, u32[]{:S(2)}) async-start(bf16[8,16,512]{2,1,0:T(8,128)(2,1)} %bitcast.5), calls=%async_computation.1 | async-start | bytes 262144 | tf_op jit(solution)/shard_map/all_to_all | solution.py:428
  48.3 4.8 %copy-start.6 = (f32[1,32,1024]{2,1,0:T(8,128)S(1)}, f32[1,32,1024]{2,1,0:T(8,128)}, u32[]{:S(2)}) copy-start(f32[1,32,1024]{2,1,0:T(8,128)} %get-tuple-element.54) | copy-start | bytes 393220
  48.3 9.5 %copy-start.5 = (f32[1,32,1024]{2,1,0:T(8,128)S(1)}, f32[1,32,1024]{2,1,0:T(8,128)}, u32[]{:S(2)}) copy-start(f32[1,32,1024]{2,1,0:T(8,128)} %get-tuple-element.42) | copy-start | bytes 393220
  49.4 23.0 %all-to-all-start.2 = ((bf16[8,16,2688]{2,1,0:T(8,128)(2,1)}), bf16[8,16,2688]{2,1,0:T(8,128)(2,1)S(1)}, u32[]{:S(2)}, u32[]{:S(2)}) async-start(bf16[8,16,2688]{2,1,0:T(8,128)(2,1)} %bitcast.6), calls=%async_computation.2 | async-start | bytes 1376256 | tf_op jit(solution)/shard_map/all_to_all | solution.py:428
  53.1 19.3 %copy-start.4 = (f32[2,1024]{1,0:T(2,128)S(1)}, f32[2,1024]{1,0:T(2,128)}, u32[]{:S(2)}) copy-start(f32[2,1024]{1,0:T(2,128)} %get-tuple-element.26.coef_ref) | copy-start | bytes 24580
  54.2 3.9 %collective-permute-start.4 = (bf16[16,512]{1,0:T(8,128)(2,1)S(1)}, bf16[16,512]{1,0:T(8,128)(2,1)S(1)}, u32[]{:S(2)}, u32[]{:S(2)}) collective-permute-start(bf16[16,512]{1,0:T(8,128)(2,1)S(1)} %get-tuple-element.25.refs_0_), channel_id=1, source_target_pairs={{0,1},{1,2},{2,3},{3,0},{4,5},{5,6},{6,7},{7,4},{8,9},{9,10},{10,1... | collective-permute-start | bytes 49160 | tf_op jit(solution)/shard_map/ppermute | solution.py:537
  55.1 4.1 %collective-permute-start.5 = (bf16[16,512]{1,0:T(8,128)(2,1)S(1)}, bf16[16,512]{1,0:T(8,128)(2,1)S(1)}, u32[]{:S(2)}, u32[]{:S(2)}) collective-permute-start(bf16[16,512]{1,0:T(8,128)(2,1)S(1)} %get-tuple-element.25.refs_0_), channel_id=1, source_target_pairs={{0,2},{1,3},{2,0},{3,1},{4,6},{5,7},{6,4},{7,5},{8,10},{9,11},{10,... | collective-permute-start | bytes 49160 | tf_op jit(solution)/shard_map/ppermute | solution.py:537
  57.2 2.6 %collective-permute-start.6 = (bf16[16,512]{1,0:T(8,128)(2,1)S(1)}, bf16[16,512]{1,0:T(8,128)(2,1)S(1)}, u32[]{:S(2)}, u32[]{:S(2)}) collective-permute-start(bf16[16,512]{1,0:T(8,128)(2,1)S(1)} %get-tuple-element.25.refs_0_), channel_id=1, source_target_pairs={{0,3},{1,0},{2,1},{3,2},{4,7},{5,4},{6,5},{7,6},{8,11},{9,8},{10,9... | collective-permute-start | bytes 49160 | tf_op jit(solution)/shard_map/ppermute | solution.py:537
  59.8 6.0 %collective-permute-start.7 = (bf16[16,512]{1,0:T(8,128)(2,1)S(1)}, bf16[16,512]{1,0:T(8,128)(2,1)S(1)}, u32[]{:S(2)}, u32[]{:S(2)}) collective-permute-start(bf16[16,512]{1,0:T(8,128)(2,1)S(1)} %shard_map.129), channel_id=1, source_target_pairs={{0,32},{32,0},{1,33},{33,1},{2,34},{34,2},{3,35},{35,3},{4,36},{36... | collective-permute-start | bytes 49160 | tf_op jit(solution)/shard_map/ppermute | solution.py:561
  64.9 17.2 %copy-start = (bf16[3584,256]{1,0:T(8,128)(2,1)S(1)}, bf16[3584,256]{1,0:T(8,128)(2,1)}, u32[]{:S(2)}) copy-start(bf16[3584,256]{1,0:T(8,128)(2,1)} %down_ref.9) | copy-start | bytes 5505028
  65.7 3.1 %collective-permute-start.10 = (bf16[2,16,512]{2,1,0:T(8,128)(2,1)S(1)}, bf16[2,16,512]{2,1,0:T(8,128)(2,1)S(1)}, u32[]{:S(2)}, u32[]{:S(2)}) collective-permute-start(bf16[2,16,512]{2,1,0:T(8,128)(2,1)S(1)} %get-tuple-element.33), channel_id=1, source_target_pairs={{0,192},{64,0},{128,64},{192,128},{1,193},{65,1},{129,65},{193,129... | collective-permute-start | bytes 98312 | tf_op jit(solution)/shard_map/ppermute | solution.py:537
  66.6 4.3 %collective-permute-start.9 = (bf16[2,16,512]{2,1,0:T(8,128)(2,1)S(1)}, bf16[2,16,512]{2,1,0:T(8,128)(2,1)S(1)}, u32[]{:S(2)}, u32[]{:S(2)}) collective-permute-start(bf16[2,16,512]{2,1,0:T(8,128)(2,1)S(1)} %get-tuple-element.33), channel_id=1, source_target_pairs={{0,128},{64,192},{128,0},{192,64},{1,129},{65,193},{129,1},{193,65... | collective-permute-start | bytes 98312 | tf_op jit(solution)/shard_map/ppermute | solution.py:537
  67.8 4.5 %collective-permute-start.8 = (bf16[2,16,512]{2,1,0:T(8,128)(2,1)S(1)}, bf16[2,16,512]{2,1,0:T(8,128)(2,1)S(1)}, u32[]{:S(2)}, u32[]{:S(2)}) collective-permute-start(bf16[2,16,512]{2,1,0:T(8,128)(2,1)S(1)} %get-tuple-element.33), channel_id=1, source_target_pairs={{0,64},{64,128},{128,192},{192,0},{1,65},{65,129},{129,193},{193,1... | collective-permute-start | bytes 98312 | tf_op jit(solution)/shard_map/ppermute | solution.py:537
  75.1 16.5 %all-to-all-start.3 = ((bf16[8,16,1024]{2,1,0:T(8,128)(2,1)}), bf16[8,16,1024]{2,1,0:T(8,128)(2,1)S(1)}, u32[]{:S(2)}, u32[]{:S(2)}) async-start(bf16[8,16,1024]{2,1,0:T(8,128)(2,1)} %shard_map.131.after_ref), calls=%async_computation.3 | async-start | bytes 524288 | tf_op jit(solution)/shard_map/all_to_all | solution.py:428
  82.1 1.0 copy-start.2
  91.6 10.0 %collective-permute-start.11 = (bf16[144,896]{1,0:T(8,128)(2,1)S(1)}, bf16[144,896]{1,0:T(8,128)(2,1)S(1)}, u32[]{:S(2)}, u32[]{:S(2)}) collective-permute-start(bf16[144,896]{1,0:T(8,128)(2,1)S(1)} %shard_map.133.after_ref.own_ref), channel_id=1, source_target_pairs={{0,1},{1,2},{2,3},{3,0},{4,5},{5,6},{6,7},{7,4},{8,9},{9,10},{10,1... | collective-permute-start | bytes 774152 | tf_op jit(solution)/shard_map/ppermute | solution.py:623
  92.5 10.9 %collective-permute-start.12 = (bf16[144,896]{1,0:T(8,128)(2,1)S(1)}, bf16[144,896]{1,0:T(8,128)(2,1)S(1)}, u32[]{:S(2)}, u32[]{:S(2)}) collective-permute-start(bf16[144,896]{1,0:T(8,128)(2,1)S(1)} %shard_map.133.after_ref.own_ref), channel_id=1, source_target_pairs={{0,2},{1,3},{2,0},{3,1},{4,6},{5,7},{6,4},{7,5},{8,10},{9,11},{10,... | collective-permute-start | bytes 774152 | tf_op jit(solution)/shard_map/ppermute | solution.py:623
  95.2 9.0 %collective-permute-start.13 = (bf16[144,896]{1,0:T(8,128)(2,1)S(1)}, bf16[144,896]{1,0:T(8,128)(2,1)S(1)}, u32[]{:S(2)}, u32[]{:S(2)}) collective-permute-start(bf16[144,896]{1,0:T(8,128)(2,1)S(1)} %shard_map.133.after_ref.own_ref), channel_id=1, source_target_pairs={{0,3},{1,0},{2,1},{3,2},{4,7},{5,4},{6,5},{7,6},{8,11},{9,8},{10,9... | collective-permute-start | bytes 774152 | tf_op jit(solution)/shard_map/ppermute | solution.py:623
  (1 other events, 0.9 us)
